TPU v7x, 32 devices: a whole 2x2x4 slice. The times are simulated.
32 devices in a mesh: dp: 16 (over z, x, core), tensor: 2 (over y).
Axes of the slice: x: 2, y: 2, z: 4, core: 2. Of those that a mesh axis runs over, the one named last changes fastest.
Arguments:
- hidden: bfloat16 [8192, 768], P('dp'), may hold values from -6 to 6
- lengths: int32 [16], P('dp'), may hold values from 128 to 512, as said below
- attn_in: bfloat16 [3, 768, 768], P(None, None, 'tensor'), may hold values from -0.21875 to 0.21875
- attn_in_bias: bfloat16 [2, 768], P(None, 'tensor'), may hold values from -0.59765625 to 0.59765625
- rel_table: bfloat16 [320, 64], replicated, may hold values from -6 to 6
- attn_out: bfloat16 [768, 768], P('tensor'), may hold values from -2.5 to 2.5
- attn_out_bias: bfloat16 [768], replicated, may hold values from -1 to 1
- norm1_gain: bfloat16 [768], replicated, may hold values from 0.5 to 1.5
- norm1_bias: bfloat16 [768], replicated, may hold values from -1 to 1
- norm2_gain: bfloat16 [768], replicated, may hold values from 0.5 to 1.5
- norm2_bias: bfloat16 [768], replicated, may hold values from -1 to 1
- ffn_in: bfloat16 [768, 3072], P(None, 'tensor'), may hold values from -0.21875 to 0.21875
- ffn_in_bias: bfloat16 [3072], P('tensor'), may hold values from -3 to 3
- ffn_out: bfloat16 [3072, 768], P('tensor'), may hold values from -0.109375 to 0.109375
- ffn_out_bias: bfloat16 [768], replicated, may hold values from -1 to 1
- cotangent: bfloat16 [8192, 768], P('dp'), may hold values from -6 to 6
Outputs:
- output: bfloat16 [8192, 768], P('dp')
- grad_hidden: bfloat16 [8192, 768], P('dp')
- grad_attn_in: float32 [3, 768, 768], P(None, 'dp', 'tensor')
- grad_attn_in_bias: float32 [2, 768], P(None, 'tensor')
- grad_rel_table: float32 [320, 64], replicated
- grad_attn_out: float32 [768, 768], P('tensor', 'dp')
- grad_attn_out_bias: float32 [768], replicated
- grad_norm1_gain: float32 [768], replicated
- grad_norm1_bias: float32 [768], replicated
- grad_norm2_gain: float32 [768], replicated
- grad_norm2_bias: float32 [768], replicated
- grad_ffn_in: float32 [768, 3072], P('dp', 'tensor')
- grad_ffn_in_bias: float32 [3072], P('tensor')
- grad_ffn_out: float32 [3072, 768], P('tensor', 'dp')
- grad_ffn_out_bias: float32 [768], replicated
Inputs may be any that keep to these rules, and one draw needn't show every extreme that they name: Each sequence has 512 slots, the first lengths of them frames and the rest padding; speech sequences and shorter text sequences are mixed unevenly, and at least one sequence fills all its slots.
All inputs are finite; a program needn't handle non-finite values.
Results may differ from a plain program's by a relative error of at most 0.013.
Values sent between devices are 32-bit elements; how exact they have to be, the bound alone decides.
A program may use at most 192 MiB of HBM per device.

v0:
```python
from functools import partial

import jax
import jax.numpy as jnp
from jax import lax
from jax.experimental import pallas as pl
from jax.experimental.pallas import tpu as pltpu
from jax.sharding import PartitionSpec as P

HD = 64
EPSILON = 1e-05
NEGATIVE = -1e30
SQRT_HALF = 0.7071067811865476
INV_SQRT_2PI = 0.3989422804014327
RB = 128
RF = 256
CW = 384
SLOTS = 4
MESH = pl.DeviceIdType.MESH
F32 = jnp.float32
BF16 = jnp.bfloat16


def mm(a, b):
    return jnp.dot(a, b, preferred_element_type=F32)


def mm_nt(a, b):
    return lax.dot_general(a, b, (((1,), (1,)), ((), ())), preferred_element_type=F32)


def mm_tn(a, b):
    return lax.dot_general(a, b, (((0,), (0,)), ((), ())), preferred_element_type=F32)


def norm_stats(value):
    mean = jnp.mean(value, axis=-1, keepdims=True)
    centred = value - mean
    scale = lax.rsqrt(jnp.mean(centred * centred, axis=-1, keepdims=True) + EPSILON)
    return centred * scale, scale


def norm_back(grad, unit, scale, gain):
    grad_unit = grad * gain
    inner = (
        grad_unit
        - jnp.mean(grad_unit, axis=-1, keepdims=True)
        - unit * jnp.mean(grad_unit * unit, axis=-1, keepdims=True)
    )
    return inner * scale


def col_sum(value):
    return jnp.sum(value, axis=0, keepdims=True)


def lanes_of(ref3, rows):
    return jnp.concatenate([ref3[p, rows, :] for p in range(ref3.shape[0])], axis=1)


V_N1G, V_N1B, V_REL, V_AOB, V_N2G, V_N2B, V_FOB, V_FIB, V_AIB = 0, 6, 16, 176, 182, 188, 194, 200, 212
YROWS, VROWS = 176, 224


def body(
    ring,
    hidden, lengths, attn_in, rel_table, attn_out, vectors_in, ffn_in, ffn_out, cotangent,
    output, grad_hidden, g_attn_in, g_attn_out, g_ffn_in, g_ffn_out, g_vec,
    *scratch,
):
    names = SCRATCH_RING if ring else SCRATCH_PLAIN + ("g_full",)
    s = dict(zip(names, scratch))
    slots, width = hidden.shape
    local = attn_out.shape[0]
    pairs = local // 128
    units = ffn_in.shape[1]
    table_rows = rel_table.shape[0]
    reach = table_rows // 2
    blocks = slots // RB
    ext = slots + RB
    head_scale = HD ** (-0.5)

    dp = lax.axis_index("dp")
    ten = lax.axis_index("tensor")
    y_peer = (dp, 1 - ten)
    if ring:
        core = lax.rem(dp, 2)
        x_at = lax.rem(lax.div(dp, 2), 2)
        z_at = lax.div(dp, 4)
        core_peer = (dp + 1 - 2 * core, ten)
        x_peer = (dp + 2 - 4 * x_at, ten)
        z_peers = [(lax.rem(dp + 4 * d, 16), ten) for d in (1, 2, 3)]
        greet = [y_peer, core_peer, x_peer] + z_peers
    else:
        greet = [y_peer]

    barrier = pltpu.get_barrier_semaphore()
    for peer in greet:
        pl.semaphore_signal(barrier, inc=1, device_id=peer, device_id_type=MESH)
    pl.semaphore_wait(barrier, len(greet))

    def remote(src, dst, name, at, peer):
        return pltpu.make_async_remote_copy(
            src_ref=src, dst_ref=dst, send_sem=s[name + "_s"].at[at], recv_sem=s[name + "_r"].at[at],
            device_id=peer, device_id_type=MESH,
        )

    if ring:
        piece = local // 4
        mine = 2 * x_at + core
        s["wo_stage"][...] = attn_out[pl.ds(pl.multiple_of(mine * piece, 16), piece), :].astype(F32)
        wo_y = remote(s["wo_stage"], s["wo_recv"].at[mine], "wo", 0, y_peer)
        wo_x = remote(s["wo_recv"].at[mine], s["wo_recv"].at[mine], "wo", 1, x_peer)
        other = 2 * (1 - x_at) + core
        wo_c0 = remote(s["wo_recv"].at[mine], s["wo_recv"].at[mine], "wo", 2, core_peer)
        wo_c1 = remote(s["wo_recv"].at[other], s["wo_recv"].at[other], "wo", 3, core_peer)
    else:
        s["wo_stage"][...] = attn_out[...].astype(F32)
        wo_y = remote(s["wo_stage"], s["wo_recv"], "wo", 0, y_peer)
    wo_y.start()

    bias_q = vectors_in[8:9, 0:local]
    bias_v = vectors_in[8:9, local : 2 * local]
    attn_out_bias = vectors_in[0:1, :]
    gain1, offset1 = vectors_in[1:2, :], vectors_in[2:3, :]
    gain2, offset2 = vectors_in[3:4, :], vectors_in[4:5, :]
    ffn_out_bias = vectors_in[5:6, :]
    seq_len = lengths[0]

    ext_rows = 2 * slots
    distance = slots - 1 - lax.broadcasted_iota(jnp.int32, (ext_rows, table_rows), 0)
    bucket = jnp.clip(distance, -reach, reach - 1) + reach
    pick = (bucket == lax.broadcasted_iota(jnp.int32, (ext_rows, table_rows), 1)).astype(BF16)
    rel = rel_table[...]
    s["table"][...] = mm(pick, jnp.concatenate([rel, rel], axis=1)).astype(BF16)

    def project(i, carry):
        rows = pl.ds(pl.multiple_of(i * RF, RF), RF)
        unit, unused = norm_stats(hidden[rows, :].astype(F32))
        normed = (unit * gain1 + offset1).astype(BF16)
        s["normed_t"][i] = normed.T
        q = ((mm(normed, attn_in[0]) + bias_q) * head_scale).astype(BF16)
        k = mm(normed, attn_in[1]).astype(BF16)
        v = (mm(normed, attn_in[2]) + bias_v).astype(BF16)
        for p in range(pairs):
            s["q"][p, rows, :] = q[:, p * 128 : (p + 1) * 128]
            s["k"][p, rows, :] = k[:, p * 128 : (p + 1) * 128]
            s["v"][p, rows, :] = v[:, p * 128 : (p + 1) * 128]
        return carry

    lax.fori_loop(0, slots // RF, project, 0)

    low_lanes = lax.broadcasted_iota(jnp.int32, (RB, 128), 1) < HD
    key_ok = lax.broadcasted_iota(jnp.int32, (1, slots), 1) < seq_len

    def stack(both):
        zero = jnp.zeros_like(both)
        return jnp.concatenate([jnp.where(low_lanes, both, zero), jnp.where(low_lanes, zero, both)], axis=0)

    def unstack(tall):
        return jnp.where(low_lanes, tall[:RB], tall[RB:])

    def table_rows_of(i):
        return pl.ds(pl.multiple_of(slots - RB - i * RB, RB), ext)

    def ctx_copy(i):
        rows = pl.ds(pl.multiple_of(i * RB, RB), RB)
        return remote(s["ctx_send"].at[:, rows], s["ctx_recv"].at[:, rows], "ctx", i, y_peer)

    def attend(i, carry):
        rows = pl.ds(pl.multiple_of(i * RB, RB), RB)

        def pair_step(p, carry):
            qs = stack(s["q"][p, rows, :])
            spread = mm_nt(qs, s["table"][table_rows_of(i), :])
            shift = ext - RB + 1
            bias = jnp.concatenate(
                [
                    pltpu.roll(spread[:RB], shift, 1, stride=1, stride_axis=0)[:, :slots],
                    pltpu.roll(spread[RB:], shift, 1, stride=1, stride_axis=0)[:, :slots],
                ],
                axis=0,
            )
            scores = jnp.where(key_ok, mm_nt(qs, s["k"][p]) + bias, NEGATIVE)
            expon = jnp.exp(scores - jnp.max(scores, axis=-1, keepdims=True))
            shares = (expon * (1.0 / jnp.sum(expon, axis=-1, keepdims=True))).astype(BF16)
            s["probs"][p, i] = shares
            context = unstack(mm(shares, s["v"][p])).astype(BF16)
            s["ctx"][ten * pairs + p, rows, :] = context
            s["ctx_send"][p, rows, :] = context.astype(F32)
            return carry

        lax.fori_loop(0, pairs, pair_step, 0)
        ctx_copy(i).start()
        return carry

    lax.fori_loop(0, blocks, attend, 0)

    half = pl.ds(pl.multiple_of(ten * local, 128), local)
    far_half = pl.ds(pl.multiple_of((1 - ten) * local, 128), local)
    s["wo"][half, :] = attn_out[...]
    wo_y.wait_recv()
    if ring:
        wo_x.start()
        wo_c0.start()
        wo_x.wait_recv()
        wo_c1.start()
        wo_c0.wait_recv()
        wo_c1.wait_recv()
        for k in range(4):
            rows = pl.ds(pl.multiple_of((1 - ten) * local + k * piece, 16), piece)
            s["wo"][rows, :] = s["wo_recv"][k].astype(BF16)
    else:
        s["wo"][far_half, :] = s["wo_recv"][...].astype(BF16)

    def valid_rows(start, count):
        return (lax.broadcasted_iota(jnp.int32, (count, 1), 0) + start < seq_len).astype(F32)

    def sum_copy(name, i):
        rows = pl.ds(pl.multiple_of(i * RB, RB), RB)
        return remote(s[name + "_send"].at[rows], s[name + "_recv"].at[rows], name, i, y_peer)

    g_vec_acc = s["vec"]
    g_vec_acc[...] = jnp.zeros_like(g_vec_acc)
    s["fib"][...] = jnp.zeros_like(s["fib"])
    s["fob"][...] = jnp.zeros_like(s["fob"])
    s["aob"][...] = jnp.zeros_like(s["aob"])
    s["n1"][...] = jnp.zeros_like(s["n1"])
    s["n2"][...] = jnp.zeros_like(s["n2"])

    step_units = 512

    def feed(b, carry):
        start = pl.multiple_of(b * RF, RF)
        rows = pl.ds(start, RF)
        for j in range(RF // RB):
            ctx_copy(b * (RF // RB) + j).wait_recv()
        for p in range(pairs):
            s["ctx"][(1 - ten) * pairs + p, rows, :] = s["ctx_recv"][p, rows, :].astype(BF16)
        attended = mm(lanes_of(s["ctx"], rows), s["wo"][...]) + attn_out_bias
        middle = hidden[rows, :].astype(F32) + attended
        s["middle"][rows, :] = middle
        unit, unused = norm_stats(middle)
        normed = (unit * gain2 + offset2).astype(BF16)
        s["normed2_t"][b] = normed.T
        top = cotangent[rows, :].astype(F32) * valid_rows(start, RF)
        s["fob"][...] += col_sum(top)
        top = top.astype(BF16)
        s["top_t"][b] = top.T
        for c in range(units // step_units):
            cols = slice(c * step_units, (c + 1) * step_units)
            pre = mm(normed, ffn_in[:, cols]) + s["ffn_in_bias"][:, cols]
            share = 0.5 + 0.5 * lax.erf(pre * SQRT_HALF)
            active = (pre * share).astype(BF16)
            s["active"][rows, cols] = active
            slope = share + pre * (jnp.exp(-0.5 * pre * pre) * INV_SQRT_2PI)
            grad_pre = (mm_nt(top, ffn_out[cols, :]) * slope).astype(BF16)
            s["grad_pre"][rows, cols] = grad_pre
            s["fib"][:, cols] += col_sum(grad_pre.astype(F32))
            back = mm_nt(grad_pre, ffn_in[:, cols])
            onward = mm(active, ffn_out[cols, :])
            if c == 0:
                s["gn2_send"][rows, :] = back
                s["out_send"][rows, :] = onward
            else:
                s["gn2_send"][rows, :] += back
                s["out_send"][rows, :] += onward
        for j in range(RF // RB):
            sum_copy("gn2", b * (RF // RB) + j).start()
        return carry

    s["ffn_in_bias"][:, 0:width] = vectors_in[6:7, :]
    s["ffn_in_bias"][:, width : 2 * width] = vectors_in[7:8, :]
    lax.fori_loop(0, slots // RF, feed, 0)

    def grad_chunk(left_t, right):
        total = mm(left_t[0], right[0:RF])
        for b in range(1, slots // RF):
            total += mm(left_t[b], right[b * RF : (b + 1) * RF])
        return total

    ffn_chunks = 2 * units // CW
    attn_chunks = 4

    def keep(total, chunk, slot):
        if ring:
            parts = total.reshape(8, 2, 48, CW)
            even, odd = parts[:, 0], parts[:, 1]
            s["g_own"][chunk] = jnp.where(core == 0, even, odd).reshape(4, 2, 48, CW)
            s["g_send"][slot] = jnp.where(core == 0, odd, even).reshape(4, 2, 48, CW)
            core_copy(chunk, slot).start()
        else:
            s["g_full"][chunk] = total

    def core_copy(chunk, slot):
        return remote(s["g_send"].at[slot], s["core_recv"].at[slot], "gc", chunk, core_peer)

    def x_copy(chunk):
        return remote(s["g_own"].at[chunk, :, 1 - x_at], s["x_recv"].at[chunk], "gx", chunk, x_peer)

    def z_copies(chunk):
        return [
            remote(
                s["g_own"].at[chunk, lax.rem(z_at + d, 4), x_at], s["z_recv"].at[chunk, 3 - d],
                "gz", 3 * chunk + 3 - d, z_peers[d - 1],
            )
            for d in (1, 2, 3)
        ]

    def core_done(chunk, slot):
        core_copy(chunk, slot).wait_recv()
        s["g_own"][chunk] = s["g_own"][chunk] + s["core_recv"][slot]
        x_copy(chunk).start()

    def x_done(chunk):
        x_copy(chunk).wait_recv()
        for z in range(4):
            s["g_own"][chunk, z, x_at] = s["g_own"][chunk, z, x_at] + s["x_recv"][chunk, z]
        for copy in z_copies(chunk):
            copy.start()

    def z_done(chunk):
        for copy in z_copies(chunk):
            copy.wait_recv()
        part = s["g_own"][chunk, z_at, x_at]
        for d in range(3):
            part += s["z_recv"][chunk, d]
        return part

    def out_grad(c, carry):
        cols = pl.ds(pl.multiple_of(c * CW, CW), CW)
        keep(grad_chunk(s["top_t"], s["active"].at[:, cols]), c, c)
        return carry

    def in_grad(c, carry):
        cols = pl.ds(pl.multiple_of(c * CW, CW), CW)
        keep(grad_chunk(s["normed2_t"], s["grad_pre"].at[:, cols]), c + units // CW, c)
        return carry

    def group_done(first):
        lax.fori_loop(0, SLOTS, lambda c, carry: (core_done(first + c, c), carry)[1], 0)

    def next_group(first):
        pl.semaphore_signal(s["free"].at[0], inc=1, device_id=core_peer, device_id_type=MESH)
        lax.fori_loop(0, SLOTS, lambda c, carry: (core_copy(first + c, c).wait_send(), carry)[1], 0)
        pl.semaphore_wait(s["free"].at[0], 1)

    lax.fori_loop(0, units // CW, out_grad, 0)
    if ring:
        group_done(0)
        next_group(0)
    lax.fori_loop(0, units // CW, in_grad, 0)
    if ring:
        group_done(SLOTS)

    s["grad_k"][...] = jnp.zeros_like(s["grad_k"])
    s["grad_v"][...] = jnp.zeros_like(s["grad_v"])
    s["grad_table"][...] = jnp.zeros_like(s["grad_table"])
    flip_row = lax.broadcasted_iota(jnp.int32, (2 * RB, 2 * RB), 0)
    flip_col = lax.broadcasted_iota(jnp.int32, (2 * RB, 2 * RB), 1)
    same_half = (flip_row < RB) == (flip_col < RB)
    local_row = lax.rem(flip_row, RB)
    local_col = lax.rem(flip_col, RB)
    flip = (same_half & (local_row + local_col == RB - 1)).astype(BF16)

    def attend_back(i, carry):
        start = pl.multiple_of(i * RB, RB)
        rows = pl.ds(start, RB)
        sum_copy("gn2", i).wait_recv()
        grad_normed = s["gn2_send"][rows, :] + s["gn2_recv"][rows, :]
        unit, scale = norm_stats(s["middle"][rows, :])
        s["n2"][0:1, :] += col_sum(grad_normed * unit)
        s["n2"][1:2, :] += col_sum(grad_normed)
        top = cotangent[rows, :].astype(F32) * valid_rows(start, RB)
        grad_middle = top + norm_back(grad_normed, unit, scale, gain2)
        s["grad_middle"][rows, :] = grad_middle
        grad_attended = grad_middle.astype(BF16)
        s["aob"][...] += col_sum(grad_attended.astype(F32))
        s["wo"][:, pl.ds(start, RB)] = grad_attended.T
        grad_context = mm_nt(grad_attended, attn_out[...]).astype(BF16)
        for p in range(pairs):
            s["grad_ctx"][p] = grad_context[:, p * 128 : (p + 1) * 128]

        def pair_step(p, carry):
            qs = stack(s["q"][p, rows, :])
            gs = stack(s["grad_ctx"][p])
            low = s["probs"][p, i]
            s["grad_v"][p] += mm_tn(low, gs)
            shares = low.astype(F32)
            grad_shares = mm_nt(gs, s["v"][p])
            inner = jnp.sum(grad_shares * shares, axis=-1, keepdims=True)
            grad_scores = (shares * (grad_shares - inner)).astype(BF16)
            s["grad_k"][p] += mm_tn(grad_scores, qs)
            grad_q = mm(grad_scores, s["k"][p])
            flipped = mm(flip, grad_scores)
            wide = jnp.concatenate([flipped, jnp.zeros((2 * RB, RB), F32)], axis=1)
            spread = jnp.concatenate(
                [
                    pltpu.roll(wide[:RB], 0, 1, stride=1, stride_axis=0),
                    pltpu.roll(wide[RB:], 0, 1, stride=1, stride_axis=0),
                ],
                axis=0,
            ).astype(BF16)
            q_flipped = mm(flip, qs).astype(BF16)
            s["grad_table"][table_rows_of(i), :] += mm_tn(spread, q_flipped)
            turned = mm(spread, s["table"][table_rows_of(i), :])
            high = turned.astype(BF16)
            rest = (turned - high.astype(F32)).astype(BF16)
            grad_q = unstack(grad_q + (mm(flip, high) + mm(flip, rest))).astype(BF16)
            cols = pl.ds(pl.multiple_of(p * 128, 128), 128)
            s["grad_pre"][rows, cols] = (grad_q.astype(F32) * head_scale).astype(BF16)
            return carry

        lax.fori_loop(0, pairs, pair_step, 0)
        if ring:
            x_done(i)
        return carry

    lax.fori_loop(0, blocks, attend_back, 0)
    pl.semaphore_signal(s["free"].at[1], inc=1, device_id=y_peer, device_id_type=MESH)

    def send_out(i, carry):
        sum_copy("out", i).start()
        return carry

    lax.fori_loop(0, blocks, send_out, 0)

    for p in range(pairs):
        at = local + p * 128
        s["grad_pre"][:, at : at + 128] = s["grad_k"][p].astype(BF16)
        at += local
        s["grad_pre"][:, at : at + 128] = s["grad_v"][p].astype(BF16)
    for i in range(blocks):
        sum_copy("gn2", i).wait_send()
    pl.semaphore_wait(s["free"].at[1], 1)

    def back_copy(i):
        rows = pl.ds(pl.multiple_of(i * RB, RB), RB)
        return remote(s["gn2_send"].at[rows], s["gn2_recv"].at[rows], "gn1", i, y_peer)

    def project_back(b, carry):
        start = pl.multiple_of(b * RF, RF)
        rows = pl.ds(start, RF)
        total = (
            mm_nt(s["grad_pre"][rows, 0:local], attn_in[0])
            + mm_nt(s["grad_pre"][rows, local : 2 * local], attn_in[1])
            + mm_nt(s["grad_pre"][rows, 2 * local : 3 * local], attn_in[2])
        )
        s["gn2_send"][rows, :] = total
        for j in range(RF // RB):
            back_copy(b * (RF // RB) + j).start()
        unit, unused = norm_stats(hidden[rows, :].astype(F32))
        s["n1"][0:1, :] += col_sum(total * unit)
        s["n1"][1:2, :] += col_sum(total)
        return carry

    lax.fori_loop(0, slots // RF, project_back, 0)

    if ring:
        next_group(SLOTS)

    def attn_grad(which, carry):
        cols = pl.ds(pl.multiple_of(which * local, 128), local)
        keep(grad_chunk(s["normed_t"], s["grad_pre"].at[:, cols]), ffn_chunks + which, which)
        return carry

    lax.fori_loop(0, 3, attn_grad, 0)
    context = jnp.concatenate([s["ctx"][ten * pairs + p] for p in range(pairs)], axis=1)
    keep(mm(s["wo"][:, 0:slots], context), ffn_chunks + 3, 3)

    def put(at, row):
        for j in range(row.shape[1] // 128):
            g_vec_acc[at + j : at + j + 1, :] = row[:, j * 128 : (j + 1) * 128]

    put(V_N1G, s["n1"][0:1, :])
    put(V_N1B, s["n1"][1:2, :])
    put(V_N2G, s["n2"][0:1, :])
    put(V_N2B, s["n2"][1:2, :])
    put(V_AOB, s["aob"][...])
    put(V_FOB, s["fob"][...])
    put(V_FIB, s["fib"][...])
    put(V_AIB, col_sum(s["grad_pre"][:, 0:local].astype(F32)))
    put(V_AIB + pairs, col_sum(s["grad_pre"][:, 2 * local : 3 * local].astype(F32)))
    grad_rel = lax.dot_general(
        pick.astype(F32), s["grad_table"][...], (((0,), (0,)), ((), ())),
        preferred_element_type=F32, precision=lax.Precision.HIGHEST,
    )
    grad_rel = grad_rel + pltpu.roll(grad_rel, HD, 1)
    fold = lax.broadcasted_iota(jnp.int32, (reach, 128), 1) < HD
    g_vec_acc[V_REL : V_REL + reach, :] = jnp.where(fold, grad_rel[:reach], grad_rel[reach:])

    def vec_step(step, peer, count):
        rows = pl.ds(0, count)
        return remote(s["vec_send"].at[step, rows], s["vec_recv"].at[step, rows], "vec", step, peer)

    def share(step, peer, count):
        s["vec_send"][step, 0:count] = g_vec_acc[0:count, :]
        vec_step(step, peer, count).start()

    def merge(step, peer, count):
        vec_step(step, peer, count).wait_recv()
        g_vec_acc[0:count, :] = s["vec_send"][step, 0:count] + s["vec_recv"][step, 0:count]

    if ring:
        z_low = (dp + 4 - 8 * lax.rem(z_at, 2), ten)
        z_high = (lax.rem(dp + 8, 16), ten)
        vec_peers = [core_peer, x_peer, z_low, z_high]
        share(1, core_peer, VROWS)
        group_done(ffn_chunks)
        merge(1, core_peer, VROWS)
        for step in (2, 3, 4):
            share(step, vec_peers[step - 1], VROWS)
            merge(step, vec_peers[step - 1], VROWS)
        lax.fori_loop(blocks, ffn_chunks, lambda c, carry: (x_done(c), carry)[1], 0)
    share(0, y_peer, YROWS)

    def finish_out(i, carry):
        start = pl.multiple_of(i * RB, RB)
        rows = pl.ds(start, RB)
        sum_copy("out", i).wait_recv()
        branch = s["out_send"][rows, :] + s["out_recv"][rows, :]
        total = s["middle"][rows, :] + (branch + ffn_out_bias)
        output[rows, :] = (total * valid_rows(start, RB)).astype(BF16)
        return carry

    def finish_hidden(i, carry):
        rows = pl.ds(pl.multiple_of(i * RB, RB), RB)
        back_copy(i).wait_recv()
        grad_normed = s["gn2_send"][rows, :] + s["gn2_recv"][rows, :]
        unit, scale = norm_stats(hidden[rows, :].astype(F32))
        total = s["grad_middle"][rows, :] + norm_back(grad_normed, unit, scale, gain1)
        grad_hidden[rows, :] = total.astype(BF16)
        return carry

    lax.fori_loop(0, blocks, finish_out, 0)
    if ring:
        for c in range(units // CW):
            g_ffn_out[c * CW : (c + 1) * CW, :] = z_done(c).T
        for c in range(units // CW):
            g_ffn_in[:, c * CW : (c + 1) * CW] = z_done(c + units // CW)
        lax.fori_loop(ffn_chunks, ffn_chunks + attn_chunks, lambda c, carry: (x_done(c), carry)[1], 0)
    lax.fori_loop(0, blocks, finish_hidden, 0)
    if ring:
        for c in range(3):
            g_attn_in[c] = z_done(ffn_chunks + c)
        g_attn_out[...] = z_done(ffn_chunks + 3).T
    merge(0, y_peer, YROWS)
    g_vec[...] = g_vec_acc[...]

    wo_y.wait_send()
    if ring:
        wo_x.wait_send()
        wo_c0.wait_send()
        wo_c1.wait_send()

    def sent(i, carry):
        ctx_copy(i).wait_send()
        sum_copy("out", i).wait_send()
        back_copy(i).wait_send()
        return carry

    lax.fori_loop(0, blocks, sent, 0)
    vec_step(0, y_peer, YROWS).wait_send()
    if ring:
        for step in (1, 2, 3, 4):
            vec_step(step, vec_peers[step - 1], VROWS).wait_send()

        def grads_sent(c, carry):
            x_copy(c).wait_send()
            for copy in z_copies(c):
                copy.wait_send()
            return carry

        lax.fori_loop(0, ffn_chunks + attn_chunks, grads_sent, 0)
        for c in range(SLOTS):
            core_copy(ffn_chunks + c, c).wait_send()


def scratch_of(ring, slots, width, local, units, chunks, ffn_chunks):
    pairs = local // 128
    blocks = slots // RB
    halves = slots // RF
    vm, dma = pltpu.VMEM, pltpu.SemaphoreType.DMA
    shapes = dict(
        normed_t=vm((halves, width, RF), BF16),
        q=vm((pairs, slots, 128), BF16),
        k=vm((pairs, slots, 128), BF16),
        v=vm((pairs, slots, 128), BF16),
        table=vm((2 * slots, 128), BF16),
        probs=vm((pairs, blocks, 2 * RB, slots), BF16),
        ctx=vm((2 * pairs, slots, 128), BF16),
        ctx_send=vm((pairs, slots, 128), F32),
        ctx_recv=vm((pairs, slots, 128), F32),
        wo=vm((2 * local, width), BF16),
        wo_stage=vm((local // 4 if ring else local, width), F32),
        wo_recv=vm((4, local // 4, width) if ring else (local, width), F32),
        middle=vm((slots, width), F32),
        normed2_t=vm((halves, width, RF), BF16),
        top_t=vm((halves, width, RF), BF16),
        active=vm((slots, units), BF16),
        grad_pre=vm((slots, units), BF16),
        gn2_send=vm((slots, width), F32),
        gn2_recv=vm((slots, width), F32),
        out_send=vm((slots, width), F32),
        out_recv=vm((slots, width), F32),
        grad_middle=vm((slots, width), F32),
        grad_ctx=vm((pairs, RB, 128), BF16),
        grad_k=vm((pairs, slots, 128), F32),
        grad_v=vm((pairs, slots, 128), F32),
        grad_table=vm((2 * slots, 128), F32),
        vec=vm((VROWS, 128), F32),
        vec_send=vm((5 if ring else 1, VROWS, 128), F32),
        vec_recv=vm((5 if ring else 1, VROWS, 128), F32),
        fib=vm((1, units), F32),
        fob=vm((1, width), F32),
        aob=vm((1, width), F32),
        n1=vm((2, width), F32),
        n2=vm((2, width), F32),
        ffn_in_bias=vm((1, units), F32),
        free=pltpu.SemaphoreType.REGULAR((2,)),
        wo_s=dma((4,)), wo_r=dma((4,)),
        ctx_s=dma((blocks,)), ctx_r=dma((blocks,)),
        gn2_s=dma((blocks,)), gn2_r=dma((blocks,)),
        gn1_s=dma((blocks,)), gn1_r=dma((blocks,)),
        out_s=dma((blocks,)), out_r=dma((blocks,)),
        vec_s=dma((5,)), vec_r=dma((5,)),
    )
    if ring:
        shapes.update(
            g_own=vm((chunks, 4, 2, 48, CW), F32),
            g_send=vm((SLOTS, 4, 2, 48, CW), F32),
            core_recv=vm((SLOTS, 4, 2, 48, CW), F32),
            x_recv=vm((chunks, 4, 48, CW), F32),
            z_recv=vm((chunks, 3, 48, CW), F32),
            gc_s=dma((chunks,)), gc_r=dma((chunks,)),
            gx_s=dma((chunks,)), gx_r=dma((chunks,)),
            gz_s=dma((3 * chunks,)), gz_r=dma((3 * chunks,)),
        )
    return shapes


SCRATCH_PLAIN = tuple(scratch_of(False, 512, 768, 384, 1536, 12, 8))
SCRATCH_RING = tuple(scratch_of(True, 512, 768, 384, 1536, 12, 8))


def on_device(
    ring,
    hidden, lengths, attn_in, attn_in_bias, rel_table, attn_out, attn_out_bias,
    norm1_gain, norm1_bias, norm2_gain, norm2_bias,
    ffn_in, ffn_in_bias, ffn_out, ffn_out_bias, cotangent,
):
    slots, width = hidden.shape
    local = attn_out.shape[0]
    units = ffn_in.shape[1]
    ffn_chunks = 2 * units // CW
    chunks = ffn_chunks + 4
    vectors_in = jnp.concatenate(
        [
            attn_out_bias, norm1_gain, norm1_bias, norm2_gain, norm2_bias, ffn_out_bias,
            ffn_in_bias, attn_in_bias.reshape(2 * local),
        ]
    ).astype(F32).reshape(9, width)
    rows = width // 16
    outs = [
        jax.ShapeDtypeStruct((slots, width), BF16),
        jax.ShapeDtypeStruct((slots, width), BF16),
        jax.ShapeDtypeStruct((3, rows, local), F32),
        jax.ShapeDtypeStruct((local, rows), F32),
        jax.ShapeDtypeStruct((rows, units), F32),
        jax.ShapeDtypeStruct((units, rows), F32),
        jax.ShapeDtypeStruct((VROWS, 128), F32),
    ]
    shapes = scratch_of(ring, slots, width, local, units, chunks, ffn_chunks)
    if not ring:
        outs.append(jax.ShapeDtypeStruct((chunks, width, CW), F32))
    vmem = pl.BlockSpec(memory_space=pltpu.VMEM)

    def kernel(*refs):
        if ring:
            body(ring, *refs)
        else:
            fixed = refs[:16]
            body_plain(refs[16], fixed, refs[17:])

    def body_plain(full, fixed, scratch):
        body(ring, *fixed, *scratch, full)

    results = pl.pallas_call(
        kernel,
        out_shape=outs,
        in_specs=[vmem, pl.BlockSpec(memory_space=pltpu.SMEM)] + [vmem] * 7,
        out_specs=[vmem] * len(outs),
        scratch_shapes=list(shapes.values()),
        compiler_params=pltpu.CompilerParams(
            collective_id=0, has_side_effects=True, vmem_limit_bytes=64 * 1024 * 1024
        ),
    )(hidden, lengths, attn_in, rel_table, attn_out, vectors_in, ffn_in, ffn_out, cotangent)
    output, grad_hidden, g_attn_in, g_attn_out, g_ffn_in, g_ffn_out, vec = results[:7]
    if not ring:
        full = results[7]
        per = units // CW
        wide = jnp.swapaxes(full[: 2 * per].reshape(2, per, width, CW), 1, 2).reshape(2, width, units)

        def scatter(value, dim):
            return lax.psum_scatter(value, "dp", scatter_dimension=dim, tiled=True)

        g_ffn_out = scatter(wide[0].T, 1)
        g_ffn_in = scatter(wide[1], 0)
        g_attn_in = scatter(full[2 * per : 2 * per + 3], 1)
        g_attn_out = scatter(full[2 * per + 3].T, 1)
        vec = lax.psum(vec, "dp")

    def row(at, count=width):
        return vec[at : at + count // 128].reshape(count)

    rel_pairs = vec[V_REL : V_REL + 160]
    grad_rel = jnp.concatenate([rel_pairs[:, :HD], rel_pairs[:, HD:]], axis=0)
    return (
        output, grad_hidden, g_attn_in,
        row(V_AIB).reshape(2, local), grad_rel, g_attn_out, row(V_AOB),
        row(V_N1G), row(V_N1B), row(V_N2G), row(V_N2B),
        g_ffn_in, row(V_FIB, units), g_ffn_out, row(V_FOB),
    )


def solution(mesh):
    ring = mesh.shape["dp"] == 16
    return jax.shard_map(
        partial(on_device, ring),
        mesh=mesh,
        in_specs=(
            P("dp", None), P("dp"), P(None, None, "tensor"), P(None, "tensor"), P(),
            P("tensor", None), P(), P(), P(), P(), P(),
            P(None, "tensor"), P("tensor"), P("tensor", None), P(), P("dp", None),
        ),
        out_specs=(
            P("dp", None), P("dp", None), P(None, "dp", "tensor"), P(None, "tensor"), P(),
            P("tensor", "dp"), P(), P(), P(), P(), P(),
            P("dp", "tensor"), P("tensor"), P("tensor", "dp"), P(),
        ),
        check_vma=False,
    )
```

profile of v0, /device:TPU:0, one launch (start us, length us, event | category | flops | bytes accessed | tf_op | source)
XLA Modules:
  0.0 207.6 jit_solution(2831808988407151813)
XLA Ops:
  1.3 0.7 reshape.58
  2.0 0.8 dynamic-update-slice
  2.8 0.8 dynamic-update-slice.1
  3.7 0.9 dynamic-update-slice.2
  4.5 0.9 dynamic-update-slice.3
  5.4 0.9 dynamic-update-slice.4
  6.2 0.8 dynamic-update-slice.5
  7.1 0.9 dynamic-update-slice.6
  8.0 0.7 reshape.66.refs_5_
  8.6 1.5 copy.31.refs_3_
  10.2 185.2 %shard_map.271 = (bf16[512,768]{1,0:T(8,128)(2,1)}, bf16[512,768]{1,0:T(8,128)(2,1)}, f32[3,48,384]{2,1,0:T(8,128)}, f32[384,48]{1,0:T(8,128)}, f32[48,1536]{1,0...) custom-call(bf16[512,768]{1,0:T(8,128)(2,1)} %refs_0_.1, s32[1]{0:T(128)S(6)} %copy.47.refs_1_, ...), custom_call_target="tpu_custom_call" | custom-call | tf_op jit(solution)/shard_map/pallas_call | solution.py:688
  195.3 0.0 copy-start.1
  195.4 0.0 copy-start
  195.4 1.4 slice_bitcast_fusion
  196.8 1.4 slice_bitcast_fusion.1
  198.2 0.6 reshape_reshape.3
  198.8 1.0 fusion
  199.8 0.8 copy.32
  200.6 1.7 copy.33
  202.3 2.1 %copy.34 = f32[1536,48]{0,1:T(8,128)} copy(f32[1536,48]{1,0:T(8,128)} %get-tuple-element.42) | data formatting | bytes 589824
  204.4 0.9 copy.48
  205.3 0.9 copy.49
  206.2 0.7 copy.50
  206.9 0.7 copy.51
  (9 shorter events, 0.0 us)
Async XLA Ops:
  195.3 9.1 %copy-start.1 = (bf16[512,768]{1,0:T(8,128)(2,1)S(1)}, bf16[512,768]{1,0:T(8,128)(2,1)}, u32[]{:S(2)}) copy-start(bf16[512,768]{1,0:T(8,128)(2,1)} %get-tuple-element.68) | copy-start | bytes 2359300
  195.4 9.9 %copy-start = (bf16[512,768]{1,0:T(8,128)(2,1)S(1)}, bf16[512,768]{1,0:T(8,128)(2,1)}, u32[]{:S(2)}) copy-start(bf16[512,768]{1,0:T(8,128)(2,1)} %get-tuple-element.69) | copy-start | bytes 2359300
  199.8 6.3 %copy-start.3 = (f32[3,48,384]{2,1,0:T(8,128)S(1)}, f32[3,48,384]{2,1,0:T(8,128)}, u32[]{:S(2)}) copy-start(f32[3,48,384]{2,1,0:T(8,128)} %get-tuple-element.70) | copy-start | bytes 663556
  202.3 4.6 %copy-start.2 = (f32[48,1536]{1,0:T(8,128)S(1)}, f32[48,1536]{1,0:T(8,128)}, u32[]{:S(2)}) copy-start(f32[48,1536]{1,0:T(8,128)} %get-tuple-element.79) | copy-start | bytes 884740
where the time goes:
time: 208 us
  Pallas kernels  185 us (89%)
  local copies, waits for them, and re-layouts  21 us (10%)
    pallas_call x1, Pallas kernels, on_device(): pl.pallas_call(kernel, out_shape=outs, in_specs=[vmem, pl.BlockSpec(memor...  185 us
    unnamed x23, local copies, waits for them, and re-layouts  15.2 us

commit v1 on v0

--- a/solution.py
+++ b/solution.py
@@ -63,18 +63,33 @@
 
 
 def body(
-    ring,
-    hidden, lengths, attn_in, rel_table, attn_out, vectors_in, ffn_in, ffn_out, cotangent,
-    output, grad_hidden, g_attn_in, g_attn_out, g_ffn_in, g_ffn_out, g_vec,
+    ring, names,
+    lengths, attn_in_bias, rel_table_t, attn_out_bias, norm1_gain, norm1_bias, norm2_gain, norm2_bias,
+    ffn_in_bias, ffn_out_bias, far_hidden, far_attn_in, far_attn_out, far_ffn_in, far_ffn_out, far_cotangent,
+    far_output, far_grad_hidden, far_grads, far_vec,
     *scratch,
 ):
-    names = SCRATCH_RING if ring else SCRATCH_PLAIN + ("g_full",)
     s = dict(zip(names, scratch))
+
+    def bring(at, name, far):
+        copy = pltpu.make_async_copy(far, s[name], s["in_s"].at[at])
+        copy.start()
+        return copy
+
+    bring_attn_out = bring(0, "attn_out", far_attn_out)
+    bring_hidden = bring(1, "hidden", far_hidden)
+    bring_attn_in = bring(2, "attn_in", far_attn_in)
+    bring_cotangent = bring(3, "cotangent", far_cotangent)
+    bring_ffn_in = bring(4, "ffn_in", far_ffn_in)
+    bring_ffn_out = bring(5, "ffn_out", far_ffn_out)
+    hidden, attn_in, attn_out = s["hidden"], s["attn_in"], s["attn_out"]
+    cotangent, ffn_in, ffn_out = s["cotangent"], s["ffn_in"], s["ffn_out"]
+    output, grad_hidden = s["output"], s["grad_hidden"]
     slots, width = hidden.shape
     local = attn_out.shape[0]
     pairs = local // 128
     units = ffn_in.shape[1]
-    table_rows = rel_table.shape[0]
+    table_rows = rel_table_t.shape[1]
     reach = table_rows // 2
     blocks = slots // RB
     ext = slots + RB
@@ -97,7 +112,6 @@
     barrier = pltpu.get_barrier_semaphore()
     for peer in greet:
         pl.semaphore_signal(barrier, inc=1, device_id=peer, device_id_type=MESH)
-    pl.semaphore_wait(barrier, len(greet))
 
     def remote(src, dst, name, at, peer):
         return pltpu.make_async_remote_copy(
@@ -105,34 +119,58 @@
             device_id=peer, device_id_type=MESH,
         )
 
-    if ring:
-        piece = local // 4
-        mine = 2 * x_at + core
-        s["wo_stage"][...] = attn_out[pl.ds(pl.multiple_of(mine * piece, 16), piece), :].astype(F32)
-        wo_y = remote(s["wo_stage"], s["wo_recv"].at[mine], "wo", 0, y_peer)
-        wo_x = remote(s["wo_recv"].at[mine], s["wo_recv"].at[mine], "wo", 1, x_peer)
-        other = 2 * (1 - x_at) + core
-        wo_c0 = remote(s["wo_recv"].at[mine], s["wo_recv"].at[mine], "wo", 2, core_peer)
-        wo_c1 = remote(s["wo_recv"].at[other], s["wo_recv"].at[other], "wo", 3, core_peer)
+    bring_attn_out.wait()
+    if ring:
+        piece = local // 8
+        mine, other = 2 * x_at + core, 2 * (1 - x_at) + core
+        for h in range(2):
+            at = pl.multiple_of((4 * h + mine) * piece, 16)
+            s["wo_stage"][h] = attn_out[pl.ds(at, piece), :].astype(F32)
+
+        def wo_y(h):
+            return remote(s["wo_stage"].at[h], s["wo_recv"].at[4 * h + mine], "wo", h, y_peer)
+
+        def wo_pass(h, which, at, peer):
+            part = s["wo_recv"].at[4 * h + which]
+            return remote(part, part, "wo", at + h, peer)
+
+        def wo_x(h):
+            return wo_pass(h, mine, 2, x_peer)
+
+        def wo_core(h):
+            return wo_pass(h, mine, 4, core_peer)
+
+        def wo_core_far(h):
+            return wo_pass(h, other, 6, core_peer)
     else:
         s["wo_stage"][...] = attn_out[...].astype(F32)
-        wo_y = remote(s["wo_stage"], s["wo_recv"], "wo", 0, y_peer)
-    wo_y.start()
-
-    bias_q = vectors_in[8:9, 0:local]
-    bias_v = vectors_in[8:9, local : 2 * local]
-    attn_out_bias = vectors_in[0:1, :]
-    gain1, offset1 = vectors_in[1:2, :], vectors_in[2:3, :]
-    gain2, offset2 = vectors_in[3:4, :], vectors_in[4:5, :]
-    ffn_out_bias = vectors_in[5:6, :]
+
+        def wo_y(h):
+            return remote(s["wo_stage"], s["wo_recv"], "wo", h, y_peer)
+
+    pl.semaphore_wait(barrier, len(greet))
+    wo_y(0).start()
+    if ring:
+        wo_y(1).start()
+
+    def flat(ref):
+        value = ref[...].astype(F32)
+        return jnp.concatenate([value[j : j + 1] for j in range(value.shape[0])], axis=1)
+
+    bias_q = attn_in_bias[0:1, :].astype(F32)
+    bias_v = attn_in_bias[1:2, :].astype(F32)
+    gain1, offset1 = flat(norm1_gain), flat(norm1_bias)
+    gain2, offset2 = flat(norm2_gain), flat(norm2_bias)
+    out_bias1, out_bias2 = flat(attn_out_bias), flat(ffn_out_bias)
+    s["ffn_in_bias"][...] = flat(ffn_in_bias)
     seq_len = lengths[0]
 
     ext_rows = 2 * slots
     distance = slots - 1 - lax.broadcasted_iota(jnp.int32, (ext_rows, table_rows), 0)
     bucket = jnp.clip(distance, -reach, reach - 1) + reach
     pick = (bucket == lax.broadcasted_iota(jnp.int32, (ext_rows, table_rows), 1)).astype(BF16)
-    rel = rel_table[...]
-    s["table"][...] = mm(pick, jnp.concatenate([rel, rel], axis=1)).astype(BF16)
+    rel_t = rel_table_t[...]
+    s["table"][...] = mm_nt(pick, jnp.concatenate([rel_t, rel_t], axis=0)).astype(BF16)
 
     def project(i, carry):
         rows = pl.ds(pl.multiple_of(i * RF, RF), RF)
@@ -148,6 +186,8 @@
             s["v"][p, rows, :] = v[:, p * 128 : (p + 1) * 128]
         return carry
 
+    bring_hidden.wait()
+    bring_attn_in.wait()
     lax.fori_loop(0, slots // RF, project, 0)
 
     low_lanes = lax.broadcasted_iota(jnp.int32, (RB, 128), 1) < HD
@@ -194,24 +234,40 @@
         ctx_copy(i).start()
         return carry
 
-    lax.fori_loop(0, blocks, attend, 0)
-
     half = pl.ds(pl.multiple_of(ten * local, 128), local)
     far_half = pl.ds(pl.multiple_of((1 - ten) * local, 128), local)
     s["wo"][half, :] = attn_out[...]
-    wo_y.wait_recv()
-    if ring:
-        wo_x.start()
-        wo_c0.start()
-        wo_x.wait_recv()
-        wo_c1.start()
-        wo_c0.wait_recv()
-        wo_c1.wait_recv()
-        for k in range(4):
+    attend(0, 0)
+    if ring:
+        wo_y(0).wait_recv()
+        wo_x(0).start()
+        wo_core(0).start()
+    attend(1, 0)
+    if ring:
+        wo_y(1).wait_recv()
+        wo_x(1).start()
+        wo_core(1).start()
+        wo_x(0).wait_recv()
+        wo_core_far(0).start()
+    attend(2, 0)
+    if ring:
+        wo_x(1).wait_recv()
+        wo_core_far(1).start()
+    attend(3, 0)
+
+    if ring:
+        for h in range(2):
+            wo_core(h).wait_recv()
+            wo_core_far(h).wait_recv()
+        for k in range(8):
             rows = pl.ds(pl.multiple_of((1 - ten) * local + k * piece, 16), piece)
             s["wo"][rows, :] = s["wo_recv"][k].astype(BF16)
     else:
+        wo_y(0).wait_recv()
         s["wo"][far_half, :] = s["wo_recv"][...].astype(BF16)
+    bring_cotangent.wait()
+    bring_ffn_in.wait()
+    bring_ffn_out.wait()
 
     def valid_rows(start, count):
         return (lax.broadcasted_iota(jnp.int32, (count, 1), 0) + start < seq_len).astype(F32)
@@ -237,7 +293,7 @@
             ctx_copy(b * (RF // RB) + j).wait_recv()
         for p in range(pairs):
             s["ctx"][(1 - ten) * pairs + p, rows, :] = s["ctx_recv"][p, rows, :].astype(BF16)
-        attended = mm(lanes_of(s["ctx"], rows), s["wo"][...]) + attn_out_bias
+        attended = mm(lanes_of(s["ctx"], rows), s["wo"][...]) + out_bias1
         middle = hidden[rows, :].astype(F32) + attended
         s["middle"][rows, :] = middle
         unit, unused = norm_stats(middle)
@@ -269,8 +325,6 @@
             sum_copy("gn2", b * (RF // RB) + j).start()
         return carry
 
-    s["ffn_in_bias"][:, 0:width] = vectors_in[6:7, :]
-    s["ffn_in_bias"][:, width : 2 * width] = vectors_in[7:8, :]
     lax.fori_loop(0, slots // RF, feed, 0)
 
     def grad_chunk(left_t, right):
@@ -371,6 +425,12 @@
         unit, scale = norm_stats(s["middle"][rows, :])
         s["n2"][0:1, :] += col_sum(grad_normed * unit)
         s["n2"][1:2, :] += col_sum(grad_normed)
+
+        @pl.when(i == blocks - 1)
+        def send_out():
+            for j in range(blocks):
+                sum_copy("out", j).start()
+
         top = cotangent[rows, :].astype(F32) * valid_rows(start, RB)
         grad_middle = top + norm_back(grad_normed, unit, scale, gain2)
         s["grad_middle"][rows, :] = grad_middle
@@ -419,12 +479,6 @@
     lax.fori_loop(0, blocks, attend_back, 0)
     pl.semaphore_signal(s["free"].at[1], inc=1, device_id=y_peer, device_id_type=MESH)
 
-    def send_out(i, carry):
-        sum_copy("out", i).start()
-        return carry
-
-    lax.fori_loop(0, blocks, send_out, 0)
-
     for p in range(pairs):
         at = local + p * 128
         s["grad_pre"][:, at : at + 128] = s["grad_k"][p].astype(BF16)
@@ -456,18 +510,6 @@
 
     lax.fori_loop(0, slots // RF, project_back, 0)
 
-    if ring:
-        next_group(SLOTS)
-
-    def attn_grad(which, carry):
-        cols = pl.ds(pl.multiple_of(which * local, 128), local)
-        keep(grad_chunk(s["normed_t"], s["grad_pre"].at[:, cols]), ffn_chunks + which, which)
-        return carry
-
-    lax.fori_loop(0, 3, attn_grad, 0)
-    context = jnp.concatenate([s["ctx"][ten * pairs + p] for p in range(pairs)], axis=1)
-    keep(mm(s["wo"][:, 0:slots], context), ffn_chunks + 3, 3)
-
     def put(at, row):
         for j in range(row.shape[1] // 128):
             g_vec_acc[at + j : at + j + 1, :] = row[:, j * 128 : (j + 1) * 128]
@@ -481,10 +523,13 @@
     put(V_FIB, s["fib"][...])
     put(V_AIB, col_sum(s["grad_pre"][:, 0:local].astype(F32)))
     put(V_AIB + pairs, col_sum(s["grad_pre"][:, 2 * local : 3 * local].astype(F32)))
-    grad_rel = lax.dot_general(
-        pick.astype(F32), s["grad_table"][...], (((0,), (0,)), ((), ())),
-        preferred_element_type=F32, precision=lax.Precision.HIGHEST,
-    )
+    grad_rel = None
+    rest = s["grad_table"][...]
+    for part in range(3):
+        piece16 = rest.astype(BF16)
+        term = mm_tn(pick, piece16)
+        grad_rel = term if part == 0 else grad_rel + term
+        rest = rest - piece16.astype(F32)
     grad_rel = grad_rel + pltpu.roll(grad_rel, HD, 1)
     fold = lax.broadcasted_iota(jnp.int32, (reach, 128), 1) < HD
     g_vec_acc[V_REL : V_REL + reach, :] = jnp.where(fold, grad_rel[:reach], grad_rel[reach:])
@@ -504,23 +549,32 @@
     if ring:
         z_low = (dp + 4 - 8 * lax.rem(z_at, 2), ten)
         z_high = (lax.rem(dp + 8, 16), ten)
-        vec_peers = [core_peer, x_peer, z_low, z_high]
+        vec_peers = [y_peer, core_peer, x_peer, z_low, z_high]
         share(1, core_peer, VROWS)
-        group_done(ffn_chunks)
-        merge(1, core_peer, VROWS)
-        for step in (2, 3, 4):
-            share(step, vec_peers[step - 1], VROWS)
-            merge(step, vec_peers[step - 1], VROWS)
-        lax.fori_loop(blocks, ffn_chunks, lambda c, carry: (x_done(c), carry)[1], 0)
-    share(0, y_peer, YROWS)
+
+    if ring:
+        next_group(SLOTS)
+
+    def attn_grad(which, carry):
+        cols = pl.ds(pl.multiple_of(which * local, 128), local)
+        keep(grad_chunk(s["normed_t"], s["grad_pre"].at[:, cols]), ffn_chunks + which, which)
+        return carry
+
+    lax.fori_loop(0, 3, attn_grad, 0)
+    context = jnp.concatenate([s["ctx"][ten * pairs + p] for p in range(pairs)], axis=1)
+    keep(mm(s["wo"][:, 0:slots], context), ffn_chunks + 3, 3)
+
+    def results(at, near, far):
+        return pltpu.make_async_copy(near, far, s["out_dma"].at[at])
 
     def finish_out(i, carry):
         start = pl.multiple_of(i * RB, RB)
         rows = pl.ds(start, RB)
         sum_copy("out", i).wait_recv()
         branch = s["out_send"][rows, :] + s["out_recv"][rows, :]
-        total = s["middle"][rows, :] + (branch + ffn_out_bias)
+        total = s["middle"][rows, :] + (branch + out_bias2)
         output[rows, :] = (total * valid_rows(start, RB)).astype(BF16)
+        results(i, output.at[rows], far_output.at[rows]).start()
         return carry
 
     def finish_hidden(i, carry):
@@ -530,28 +584,54 @@
         unit, scale = norm_stats(hidden[rows, :].astype(F32))
         total = s["grad_middle"][rows, :] + norm_back(grad_normed, unit, scale, gain1)
         grad_hidden[rows, :] = total.astype(BF16)
-        return carry
-
-    lax.fori_loop(0, blocks, finish_out, 0)
-    if ring:
-        for c in range(units // CW):
-            g_ffn_out[c * CW : (c + 1) * CW, :] = z_done(c).T
-        for c in range(units // CW):
-            g_ffn_in[:, c * CW : (c + 1) * CW] = z_done(c + units // CW)
-        lax.fori_loop(ffn_chunks, ffn_chunks + attn_chunks, lambda c, carry: (x_done(c), carry)[1], 0)
-    lax.fori_loop(0, blocks, finish_hidden, 0)
-    if ring:
-        for c in range(3):
-            g_attn_in[c] = z_done(ffn_chunks + c)
-        g_attn_out[...] = z_done(ffn_chunks + 3).T
-    merge(0, y_peer, YROWS)
-    g_vec[...] = g_vec_acc[...]
-
-    wo_y.wait_send()
-    if ring:
-        wo_x.wait_send()
-        wo_c0.wait_send()
-        wo_c1.wait_send()
+        results(blocks + i, grad_hidden.at[rows], far_grad_hidden.at[rows]).start()
+        return carry
+
+    def finish_grad(c, carry):
+        s["grads"][c] = z_done(c)
+        results(2 * blocks + 1 + c, s["grads"].at[c], far_grads.at[c]).start()
+        return carry
+
+    def x_range(first, last):
+        lax.fori_loop(first, last, lambda c, carry: (x_done(c), carry)[1], 0)
+
+    vec_out = results(2 * blocks, g_vec_acc, far_vec)
+    chunks = ffn_chunks + attn_chunks
+    if ring:
+        merge(1, core_peer, VROWS)
+        share(2, x_peer, VROWS)
+        group_done(ffn_chunks)
+        x_range(blocks, ffn_chunks)
+        merge(2, x_peer, VROWS)
+        share(3, z_low, VROWS)
+        x_done(ffn_chunks)
+        merge(3, z_low, VROWS)
+        share(4, z_high, VROWS)
+        x_done(ffn_chunks + 1)
+        merge(4, z_high, VROWS)
+        share(0, y_peer, YROWS)
+        lax.fori_loop(0, blocks, finish_out, 0)
+        x_range(ffn_chunks + 2, chunks)
+        lax.fori_loop(0, ffn_chunks, finish_grad, 0)
+        lax.fori_loop(0, blocks - 1, finish_hidden, 0)
+        lax.fori_loop(ffn_chunks, chunks, finish_grad, 0)
+        merge(0, y_peer, YROWS)
+        vec_out.start()
+        finish_hidden(blocks - 1, 0)
+    else:
+        share(0, y_peer, YROWS)
+        lax.fori_loop(0, blocks, finish_out, 0)
+        merge(0, y_peer, YROWS)
+        vec_out.start()
+        lax.fori_loop(0, blocks, finish_hidden, 0)
+
+    wo_y(0).wait_send()
+    if ring:
+        wo_y(1).wait_send()
+        for h in range(2):
+            wo_x(h).wait_send()
+            wo_core(h).wait_send()
+            wo_core_far(h).wait_send()
 
     def sent(i, carry):
         ctx_copy(i).wait_send()
@@ -563,7 +643,7 @@
     vec_step(0, y_peer, YROWS).wait_send()
     if ring:
         for step in (1, 2, 3, 4):
-            vec_step(step, vec_peers[step - 1], VROWS).wait_send()
+            vec_step(step, vec_peers[step], VROWS).wait_send()
 
         def grads_sent(c, carry):
             x_copy(c).wait_send()
@@ -571,9 +651,18 @@
                 copy.wait_send()
             return carry
 
-        lax.fori_loop(0, ffn_chunks + attn_chunks, grads_sent, 0)
+        lax.fori_loop(0, chunks, grads_sent, 0)
         for c in range(SLOTS):
             core_copy(ffn_chunks + c, c).wait_send()
+        lax.fori_loop(
+            0, chunks,
+            lambda c, carry: (results(2 * blocks + 1 + c, s["grads"].at[c], far_grads.at[c]).wait(), carry)[1], 0,
+        )
+    for i in range(blocks):
+        rows = slice(i * RB, (i + 1) * RB)
+        results(i, output.at[rows], far_output.at[rows]).wait()
+        results(blocks + i, grad_hidden.at[rows], far_grad_hidden.at[rows]).wait()
+    vec_out.wait()
 
 
 def scratch_of(ring, slots, width, local, units, chunks, ffn_chunks):
@@ -582,6 +671,16 @@
     halves = slots // RF
     vm, dma = pltpu.VMEM, pltpu.SemaphoreType.DMA
     shapes = dict(
+        hidden=vm((slots, width), BF16),
+        attn_in=vm((3, width, local), BF16),
+        attn_out=vm((local, width), BF16),
+        ffn_in=vm((width, units), BF16),
+        ffn_out=vm((units, width), BF16),
+        cotangent=vm((slots, width), BF16),
+        output=vm((slots, width), BF16),
+        grad_hidden=vm((slots, width), BF16),
+        in_s=dma((6,)),
+        out_dma=dma((2 * blocks + 1 + chunks,)),
         normed_t=vm((halves, width, RF), BF16),
         q=vm((pairs, slots, 128), BF16),
         k=vm((pairs, slots, 128), BF16),
@@ -592,8 +691,8 @@
         ctx_send=vm((pairs, slots, 128), F32),
         ctx_recv=vm((pairs, slots, 128), F32),
         wo=vm((2 * local, width), BF16),
-        wo_stage=vm((local // 4 if ring else local, width), F32),
-        wo_recv=vm((4, local // 4, width) if ring else (local, width), F32),
+        wo_stage=vm((2, local // 8, width) if ring else (local, width), F32),
+        wo_recv=vm((8, local // 8, width) if ring else (local, width), F32),
         middle=vm((slots, width), F32),
         normed2_t=vm((halves, width, RF), BF16),
         top_t=vm((halves, width, RF), BF16),
@@ -618,7 +717,7 @@
         n2=vm((2, width), F32),
         ffn_in_bias=vm((1, units), F32),
         free=pltpu.SemaphoreType.REGULAR((2,)),
-        wo_s=dma((4,)), wo_r=dma((4,)),
+        wo_s=dma((8,)), wo_r=dma((8,)),
         ctx_s=dma((blocks,)), ctx_r=dma((blocks,)),
         gn2_s=dma((blocks,)), gn2_r=dma((blocks,)),
         gn1_s=dma((blocks,)), gn1_r=dma((blocks,)),
@@ -632,6 +731,7 @@
             core_recv=vm((SLOTS, 4, 2, 48, CW), F32),
             x_recv=vm((chunks, 4, 48, CW), F32),
             z_recv=vm((chunks, 3, 48, CW), F32),
+            grads=vm((chunks, 48, CW), F32),
             gc_s=dma((chunks,)), gc_r=dma((chunks,)),
             gx_s=dma((chunks,)), gx_r=dma((chunks,)),
             gz_s=dma((3 * chunks,)), gz_r=dma((3 * chunks,)),
@@ -639,8 +739,34 @@
     return shapes
 
 
-SCRATCH_PLAIN = tuple(scratch_of(False, 512, 768, 384, 1536, 12, 8))
-SCRATCH_RING = tuple(scratch_of(True, 512, 768, 384, 1536, 12, 8))
+def place(
+    output_in, grad_hidden_in, grads_in, vec,
+    output, grad_hidden, g_attn_in, g_attn_in_bias, g_rel_t, g_attn_out_t, g_attn_out_bias,
+    g_norm1_gain, g_norm1_bias, g_norm2_gain, g_norm2_bias, g_ffn_in, g_ffn_in_bias, g_ffn_out_t, g_ffn_out_bias,
+):
+    per = g_ffn_in.shape[1] // CW
+    output[...] = output_in[...]
+    grad_hidden[...] = grad_hidden_in[...]
+    g_attn_in[...] = grads_in[2 * per : 2 * per + 3]
+    g_attn_out_t[...] = grads_in[2 * per + 3]
+    for c in range(per):
+        cols = slice(c * CW, (c + 1) * CW)
+        g_ffn_out_t[:, cols] = grads_in[c]
+        g_ffn_in[:, cols] = grads_in[per + c]
+    for ref, at in (
+        (g_attn_out_bias, V_AOB), (g_norm1_gain, V_N1G), (g_norm1_bias, V_N1B), (g_norm2_gain, V_N2G),
+        (g_norm2_bias, V_N2B), (g_ffn_in_bias, V_FIB), (g_ffn_out_bias, V_FOB),
+    ):
+        ref[...] = vec[at : at + ref.shape[0], :]
+    local = g_attn_in_bias.shape[1]
+    for k in range(2):
+        at = V_AIB + k * (local // 128)
+        g_attn_in_bias[k : k + 1, :] = jnp.concatenate(
+            [vec[at + j : at + j + 1, :] for j in range(local // 128)], axis=1
+        )
+    reach = g_rel_t.shape[1] // 2
+    turned = vec[V_REL : V_REL + reach, :].T
+    g_rel_t[...] = jnp.concatenate([turned[:HD], turned[HD:]], axis=1)
 
 
 def on_device(
@@ -652,72 +778,84 @@
     slots, width = hidden.shape
     local = attn_out.shape[0]
     units = ffn_in.shape[1]
+    table_rows = rel_table.shape[0]
     ffn_chunks = 2 * units // CW
     chunks = ffn_chunks + 4
-    vectors_in = jnp.concatenate(
-        [
-            attn_out_bias, norm1_gain, norm1_bias, norm2_gain, norm2_bias, ffn_out_bias,
-            ffn_in_bias, attn_in_bias.reshape(2 * local),
-        ]
-    ).astype(F32).reshape(9, width)
     rows = width // 16
-    outs = [
-        jax.ShapeDtypeStruct((slots, width), BF16),
-        jax.ShapeDtypeStruct((slots, width), BF16),
-        jax.ShapeDtypeStruct((3, rows, local), F32),
-        jax.ShapeDtypeStruct((local, rows), F32),
-        jax.ShapeDtypeStruct((rows, units), F32),
-        jax.ShapeDtypeStruct((units, rows), F32),
-        jax.ShapeDtypeStruct((VROWS, 128), F32),
-    ]
+    shape = jax.ShapeDtypeStruct
     shapes = scratch_of(ring, slots, width, local, units, chunks, ffn_chunks)
+    names = tuple(shapes)
+    outs = [shape((slots, width), BF16), shape((slots, width), BF16), shape((chunks, rows, CW), F32), shape((VROWS, 128), F32)]
+    far = pl.BlockSpec(memory_space=pl.ANY)
+    near = pl.BlockSpec(memory_space=pltpu.VMEM)
+    out_specs = [far] * 4
     if not ring:
-        outs.append(jax.ShapeDtypeStruct((chunks, width, CW), F32))
-    vmem = pl.BlockSpec(memory_space=pltpu.VMEM)
-
-    def kernel(*refs):
-        if ring:
-            body(ring, *refs)
-        else:
-            fixed = refs[:16]
-            body_plain(refs[16], fixed, refs[17:])
-
-    def body_plain(full, fixed, scratch):
-        body(ring, *fixed, *scratch, full)
+        names = ("g_full",) + names
+        outs.append(shape((chunks, width, CW), F32))
+        out_specs.append(near)
+
+    def lanes(vector):
+        return vector.reshape(vector.shape[0] // 128, 128)
+
+    def unlanes(array):
+        return array.reshape(array.shape[0] * 128)
 
     results = pl.pallas_call(
-        kernel,
+        partial(body, ring, names),
         out_shape=outs,
-        in_specs=[vmem, pl.BlockSpec(memory_space=pltpu.SMEM)] + [vmem] * 7,
-        out_specs=[vmem] * len(outs),
+        in_specs=[pl.BlockSpec(memory_space=pltpu.SMEM)] + [near] * 9 + [far] * 6,
+        out_specs=out_specs,
         scratch_shapes=list(shapes.values()),
         compiler_params=pltpu.CompilerParams(
             collective_id=0, has_side_effects=True, vmem_limit_bytes=64 * 1024 * 1024
         ),
-    )(hidden, lengths, attn_in, rel_table, attn_out, vectors_in, ffn_in, ffn_out, cotangent)
-    output, grad_hidden, g_attn_in, g_attn_out, g_ffn_in, g_ffn_out, vec = results[:7]
-    if not ring:
-        full = results[7]
-        per = units // CW
-        wide = jnp.swapaxes(full[: 2 * per].reshape(2, per, width, CW), 1, 2).reshape(2, width, units)
-
-        def scatter(value, dim):
-            return lax.psum_scatter(value, "dp", scatter_dimension=dim, tiled=True)
-
-        g_ffn_out = scatter(wide[0].T, 1)
-        g_ffn_in = scatter(wide[1], 0)
-        g_attn_in = scatter(full[2 * per : 2 * per + 3], 1)
-        g_attn_out = scatter(full[2 * per + 3].T, 1)
-        vec = lax.psum(vec, "dp")
+    )(
+        lengths, attn_in_bias, rel_table.T, lanes(attn_out_bias), lanes(norm1_gain), lanes(norm1_bias),
+        lanes(norm2_gain), lanes(norm2_bias), lanes(ffn_in_bias), lanes(ffn_out_bias),
+        hidden, attn_in, attn_out, ffn_in, ffn_out, cotangent,
+    )
+    if ring:
+        vector = shape((width // 128, 128), F32)
+        placed = pl.pallas_call(
+            place,
+            out_shape=[
+                outs[0], outs[1], shape((3, rows, local), F32), shape((2, local), F32), shape((HD, table_rows), F32),
+                shape((rows, local), F32), vector, vector, vector, vector, vector,
+                shape((rows, units), F32), shape((units // 128, 128), F32), shape((rows, units), F32), vector,
+            ],
+            in_specs=[near] * 4,
+            out_specs=[near] * 15,
+        )(*results)
+        (
+            output, grad_hidden, g_attn_in, g_attn_in_bias, g_rel_t, g_attn_out_t, g_attn_out_bias, n1g, n1b, n2g, n2b,
+            g_ffn_in, g_ffn_in_bias, g_ffn_out_t, g_ffn_out_bias,
+        ) = placed
+        return (
+            output, grad_hidden, g_attn_in, g_attn_in_bias, g_rel_t.T, g_attn_out_t.T, unlanes(g_attn_out_bias),
+            unlanes(n1g), unlanes(n1b), unlanes(n2g), unlanes(n2b),
+            g_ffn_in, unlanes(g_ffn_in_bias), g_ffn_out_t.T, unlanes(g_ffn_out_bias),
+        )
+    output, grad_hidden, unused, vec, full = results
+    per = units // CW
+    wide = jnp.swapaxes(full[: 2 * per].reshape(2, per, width, CW), 1, 2).reshape(2, width, units)
+
+    def scatter(value, dim):
+        return lax.psum_scatter(value, "dp", scatter_dimension=dim, tiled=True)
+
+    g_ffn_out = scatter(wide[0].T, 1)
+    g_ffn_in = scatter(wide[1], 0)
+    g_attn_in = scatter(full[2 * per : 2 * per + 3], 1)
+    g_attn_out = scatter(full[2 * per + 3].T, 1)
+    vec = lax.psum(vec, "dp")
 
     def row(at, count=width):
-        return vec[at : at + count // 128].reshape(count)
-
-    rel_pairs = vec[V_REL : V_REL + 160]
+        return unlanes(vec[at : at + count // 128])
+
+    rel_pairs = vec[V_REL : V_REL + table_rows // 2]
     grad_rel = jnp.concatenate([rel_pairs[:, :HD], rel_pairs[:, HD:]], axis=0)
     return (
         output, grad_hidden, g_attn_in,
-        row(V_AIB).reshape(2, local), grad_rel, g_attn_out, row(V_AOB),
+        row(V_AIB, 2 * local).reshape(2, local), grad_rel, g_attn_out, row(V_AOB),
         row(V_N1G), row(V_N1B), row(V_N2G), row(V_N2B),
         g_ffn_in, row(V_FIB, units), g_ffn_out, row(V_FOB),
     )

time: 208 us -> 142 us (0.68)
  Pallas kernels: 185 us -> 141 us
  local copies, waits for them, and re-layouts: 21 us -> 0 us
    pallas_call x1 -> x2, Pallas kernels: 185 us -> 141 us  [the longest x1 138 us: on_device(): pl.pallas_call(partial(body, ring, names), out_shape=outs, in_specs=[pl.B...]
    unnamed x23 -> x0, local copies, waits for them, and re-layouts: 15.2 us -> none
    reshape x3 -> x0, local copies, waits for them, and re-layouts: 3.5 us -> none  [the longest x2 2.81 us: row(): return vec[at:at + count // 128].reshape(count)]
where the time goes in v1:
time: 142 us
  Pallas kernels  141 us (99%)
    pallas_call x1, Pallas kernels, on_device(): pl.pallas_call(partial(body, ring, names), out_shape=outs, in_specs=[pl.B...  138 us
    pallas_call x1, Pallas kernels, on_device(): pl.pallas_call(place, out_shape=[outs[0], outs[1], shape((3, rows, local)...  3.23 us

profile of v1, /device:TPU:0, one launch (start us, length us, event | category | flops | bytes accessed | tf_op | source)
XLA Modules:
  0.0 142.0 jit_solution(4774879672946722089)
XLA Ops:
  1.3 137.5 %shard_map.271 = (bf16[512,768]{1,0:T(8,128)(2,1)}, bf16[512,768]{1,0:T(8,128)(2,1)}, f32[12,48,384]{2,1,0:T(8,128)}, f32[224,128]{1,0:T(8,128)}) custom-call(s32[1]{0:T(128)S(6)} %copy.31.lengths, bf16[2,384]{1,0:T(2,128)(2,1)} %attn_in_bias.1, bf16[64,320]{1,0:T(8,128)(2,1)} %bitcast.18, bf16[6,128]{1,0:T(8,128)(2,1)} %bitcast.20, ...), custom_call_target="tpu_custom_call" | custom-call | tf_op jit(solution)/shard_map/pallas_call | solution.py:803
  138.8 3.2 %shard_map.272 = (bf16[512,768]{1,0:T(8,128)(2,1)}, bf16[512,768]{1,0:T(8,128)(2,1)}, f32[3,48,384]{2,1,0:T(8,128)}, f32[2,384]{1,0:T(2,128)}, f32[64,320]{1,0:T...) custom-call(bf16[512,768]{1,0:T(8,128)(2,1)} %get-tuple-element.34.o, ...), custom_call_target="tpu_custom_call" | custom-call | tf_op jit(solution)/shard_map/pallas_call | solution.py:819

commit v2 on v1

v2 whole, which is shorter than its diff:
```python
from functools import partial
from types import SimpleNamespace

import jax
import jax.numpy as jnp
from jax import lax
from jax.experimental import pallas as pl
from jax.experimental.pallas import tpu as pltpu
from jax.sharding import PartitionSpec as P

HD = 64
EPSILON = 1e-05
NEGATIVE = -1e30
SQRT_HALF = 0.7071067811865476
INV_SQRT_2PI = 0.3989422804014327
RB = 128
RF = 256
CW = 384
FULL = "g_full"
Z_FIRST = (1, 4)
SLOTS = 4
MESH = pl.DeviceIdType.MESH
F32 = jnp.float32
BF16 = jnp.bfloat16


def mm(a, b):
    return jnp.dot(a, b, preferred_element_type=F32)


def mm_nt(a, b):
    return lax.dot_general(a, b, (((1,), (1,)), ((), ())), preferred_element_type=F32)


def mm_tn(a, b):
    return lax.dot_general(a, b, (((0,), (0,)), ((), ())), preferred_element_type=F32)


def norm_stats(value):
    mean = jnp.mean(value, axis=-1, keepdims=True)
    centred = value - mean
    scale = lax.rsqrt(jnp.mean(centred * centred, axis=-1, keepdims=True) + EPSILON)
    return centred * scale, scale


def norm_back(grad, unit, scale, gain):
    grad_unit = grad * gain
    inner = (
        grad_unit
        - jnp.mean(grad_unit, axis=-1, keepdims=True)
        - unit * jnp.mean(grad_unit * unit, axis=-1, keepdims=True)
    )
    return inner * scale


def col_sum(value):
    return jnp.sum(value, axis=0, keepdims=True)


def lanes_of(ref3, rows):
    return jnp.concatenate([ref3[p, rows, :] for p in range(ref3.shape[0])], axis=1)


V_N1G, V_N1B, V_AOB, V_N2G, V_N2B, V_REL, V_FOB, V_FIB, V_AIB = 0, 6, 12, 18, 24, 32, 192, 198, 210
YROWS, VROWS = 192, 216


def body(
    ring, names,
    lengths, attn_in_bias, rel_table_t, attn_out_bias, norm1_gain, norm1_bias, norm2_gain, norm2_bias,
    ffn_in_bias, ffn_out_bias, far_hidden, far_attn_in, far_attn_out, far_ffn_in, far_ffn_out, far_cotangent,
    far_output, far_grad_hidden, far_attn_in_grad, far_attn_out_grad, far_ffn_in_grad, far_ffn_out_grad, far_vec,
    *scratch,
):
    s = SimpleNamespace(**dict(zip(names, scratch)))

    def bring(at, near, far):
        copy = pltpu.make_async_copy(far, near, s.in_s.at[at])
        copy.start()
        return copy

    bring_attn_out = bring(0, s.attn_out, far_attn_out)
    bring_hidden = bring(1, s.hidden, far_hidden)
    bring_attn_in = bring(2, s.attn_in, far_attn_in)
    hidden, attn_in, attn_out = s.hidden, s.attn_in, s.attn_out
    cotangent, ffn_in, ffn_out = s.cotangent, s.ffn_in, s.ffn_out
    output, grad_hidden = s.output, s.grad_hidden
    slots, width = hidden.shape
    local = attn_out.shape[0]
    pairs = local // 128
    units = ffn_in.shape[1]
    table_rows = rel_table_t.shape[1]
    reach = table_rows // 2
    blocks = slots // RB
    ext = slots + RB
    head_scale = HD ** (-0.5)

    dp = lax.axis_index("dp")
    ten = lax.axis_index("tensor")
    y_peer = (dp, 1 - ten)
    if ring:
        core = lax.rem(dp, 2)
        x_at = lax.rem(lax.div(dp, 2), 2)
        z_low_at = lax.rem(lax.div(dp, 4), 2)
        z_high_at = lax.div(dp, 8)
        core_peer = (dp + 1 - 2 * core, ten)
        x_peer = (dp + 2 - 4 * x_at, ten)
        z_low = (dp + 4 - 8 * z_low_at, ten)
        z_high = (dp + 8 - 16 * z_high_at, ten)
        greet = [y_peer, core_peer, x_peer, z_low, z_high]
    else:
        greet = [y_peer]

    barrier = pltpu.get_barrier_semaphore()
    for peer in greet:
        pl.semaphore_signal(barrier, inc=1, device_id=peer, device_id_type=MESH)

    def remote(src, dst, sems, at, peer):
        return pltpu.make_async_remote_copy(
            src_ref=src, dst_ref=dst, send_sem=sems.at[0, at], recv_sem=sems.at[1, at],
            device_id=peer, device_id_type=MESH,
        )

    bring_attn_out.wait()
    if ring:
        piece = local // 8
        mine = (2 * z_low_at + x_at) * 2 + core
        s.wo_stage[...] = attn_out[pl.ds(pl.multiple_of(mine * piece, 16), piece), :].astype(F32)

        def wo_y():
            return remote(s.wo_stage, s.wo_recv.at[z_low_at, x_at, core], s.wo_sem, 0, y_peer)

        def wo_pass(part, at, peer):
            return remote(part, part, s.wo_sem, at, peer)

        def wo_x():
            return wo_pass(s.wo_recv.at[z_low_at, x_at, core], 1, x_peer)

        def wo_z():
            return wo_pass(s.wo_recv.at[z_low_at, x_at, core], 2, z_low)

        def wo_xz():
            return wo_pass(s.wo_recv.at[z_low_at, 1 - x_at, core], 3, z_low)

        def wo_core(near):
            return wo_pass(s.wo_recv.at[z_low_at if near else 1 - z_low_at, :, core], 4 if near else 5, core_peer)
    else:
        s.wo_stage[...] = attn_out[...].astype(F32)

        def wo_y():
            return remote(s.wo_stage, s.wo_recv, s.wo_sem, 0, y_peer)

    pl.semaphore_wait(barrier, len(greet))
    wo_y().start()

    def flat(ref):
        value = ref[...].astype(F32)
        return jnp.concatenate([value[j : j + 1] for j in range(value.shape[0])], axis=1)

    bias_q = attn_in_bias[0:1, :].astype(F32)
    bias_v = attn_in_bias[1:2, :].astype(F32)
    gain1, offset1 = flat(norm1_gain), flat(norm1_bias)
    gain2, offset2 = flat(norm2_gain), flat(norm2_bias)
    out_bias1, out_bias2 = flat(attn_out_bias), flat(ffn_out_bias)
    s.ffn_in_bias[...] = flat(ffn_in_bias)
    seq_len = lengths[0]

    ext_rows = 2 * slots
    distance = slots - 1 - lax.broadcasted_iota(jnp.int32, (ext_rows, table_rows), 0)
    bucket = jnp.clip(distance, -reach, reach - 1) + reach
    pick = (bucket == lax.broadcasted_iota(jnp.int32, (ext_rows, table_rows), 1)).astype(BF16)
    rel_t = rel_table_t[...]
    s.table[...] = mm_nt(pick, jnp.concatenate([rel_t, rel_t], axis=0)).astype(BF16)

    def project(i, carry):
        rows = pl.ds(pl.multiple_of(i * RF, RF), RF)
        unit, unused = norm_stats(hidden[rows, :].astype(F32))
        normed = (unit * gain1 + offset1).astype(BF16)
        s.normed_t[i] = normed.T
        q = ((mm(normed, attn_in[0]) + bias_q) * head_scale).astype(BF16)
        k = mm(normed, attn_in[1]).astype(BF16)
        v = (mm(normed, attn_in[2]) + bias_v).astype(BF16)
        for p in range(pairs):
            s.q[p, rows, :] = q[:, p * 128 : (p + 1) * 128]
            s.k[p, rows, :] = k[:, p * 128 : (p + 1) * 128]
            s.v[p, rows, :] = v[:, p * 128 : (p + 1) * 128]
        return carry

    bring_hidden.wait()
    bring_attn_in.wait()
    bring_cotangent = bring(3, s.cotangent, far_cotangent)
    bring_ffn_in = bring(4, s.ffn_in, far_ffn_in)
    bring_ffn_out = bring(5, s.ffn_out, far_ffn_out)
    lax.fori_loop(0, slots // RF, project, 0)

    low_lanes = lax.broadcasted_iota(jnp.int32, (RB, 128), 1) < HD
    key_ok = lax.broadcasted_iota(jnp.int32, (1, slots), 1) < seq_len

    def stack(both):
        zero = jnp.zeros_like(both)
        return jnp.concatenate([jnp.where(low_lanes, both, zero), jnp.where(low_lanes, zero, both)], axis=0)

    def unstack(tall):
        return jnp.where(low_lanes, tall[:RB], tall[RB:])

    def table_rows_of(i):
        return pl.ds(pl.multiple_of(slots - RB - i * RB, RB), ext)

    def ctx_copy(i, p):
        rows = pl.ds(pl.multiple_of(i * RB, RB), RB)
        return remote(s.ctx_send.at[p, rows], s.ctx_recv.at[p, rows], s.ctx_sem, i * pairs + p, y_peer)

    def attend(i):
        rows = pl.ds(pl.multiple_of(i * RB, RB), RB)

        def pair_step(p, carry):
            qs = stack(s.q[p, rows, :])
            spread = mm_nt(qs, s.table[table_rows_of(i), :])
            shift = ext - RB + 1
            bias = jnp.concatenate(
                [
                    pltpu.roll(spread[:RB], shift, 1, stride=1, stride_axis=0)[:, :slots],
                    pltpu.roll(spread[RB:], shift, 1, stride=1, stride_axis=0)[:, :slots],
                ],
                axis=0,
            )
            scores = jnp.where(key_ok, mm_nt(qs, s.k[p]) + bias, NEGATIVE)
            expon = jnp.exp(scores - jnp.max(scores, axis=-1, keepdims=True))
            shares = (expon * (1.0 / jnp.sum(expon, axis=-1, keepdims=True))).astype(BF16)
            s.probs[p, i] = shares
            context = unstack(mm(shares, s.v[p])).astype(BF16)
            s.ctx[ten * pairs + p, rows, :] = context
            s.ctx_send[p, rows, :] = context.astype(F32)
            ctx_copy(i, p).start()
            return carry

        lax.fori_loop(0, pairs, pair_step, 0)

    half = pl.ds(pl.multiple_of(ten * local, 128), local)
    far_half = pl.ds(pl.multiple_of((1 - ten) * local, 128), local)
    s.wo[half, :] = attn_out[...]
    attend(0)
    if ring:
        wo_y().wait_recv()
        wo_x().start()
        wo_z().start()
    attend(1)
    if ring:
        wo_x().wait_recv()
        wo_xz().start()
        wo_core(True).start()
    attend(2)
    attend(3)

    if ring:
        wo_z().wait_recv()
        wo_xz().wait_recv()
        wo_core(False).start()
        wo_core(True).wait_recv()
        wo_core(False).wait_recv()
        s.wo[far_half, :] = s.wo_recv[...].reshape(local, width).astype(BF16)
    else:
        wo_y().wait_recv()
        s.wo[far_half, :] = s.wo_recv[...].astype(BF16)
    bring_cotangent.wait()
    bring_ffn_in.wait()
    bring_ffn_out.wait()

    def valid_rows(start, count):
        return (lax.broadcasted_iota(jnp.int32, (count, 1), 0) + start < seq_len).astype(F32)

    def gn2_copy(j):
        rows = pl.ds(pl.multiple_of((2 * j + 1 - ten) * RB, RB), RB)
        return remote(s.gn2_send.at[rows], s.gn2_recv.at[j], s.gn2_sem, j, y_peer)

    def grad_ctx_copy(j):
        return remote(s.grad_ctx_send.at[j], s.grad_ctx_recv.at[j], s.grad_ctx_sem, j, y_peer)

    def out_copy(i):
        rows = pl.ds(pl.multiple_of(i * RB, RB), RB)
        return remote(s.out_send.at[rows], s.out_recv.at[rows], s.out_sem, i, y_peer)

    g_vec_acc = s.vec
    g_vec_acc[...] = jnp.zeros_like(g_vec_acc)
    s.fib[...] = jnp.zeros_like(s.fib)
    s.fob[...] = jnp.zeros_like(s.fob)
    s.aob[...] = jnp.zeros_like(s.aob)
    s.n1[...] = jnp.zeros_like(s.n1)
    s.n2[...] = jnp.zeros_like(s.n2)

    step_units = 512

    def feed(b):
        start = b * RF
        rows = slice(start, start + RF)
        for j in range(RF // RB):
            for p in range(pairs):
                ctx_copy(b * (RF // RB) + j, p).wait_recv()
        for p in range(pairs):
            s.ctx[(1 - ten) * pairs + p, rows, :] = s.ctx_recv[p, rows, :].astype(BF16)
        attended = mm(lanes_of(s.ctx, rows), s.wo[...]) + out_bias1
        middle = hidden[rows, :].astype(F32) + attended
        s.middle[rows, :] = middle
        unit, unused = norm_stats(middle)
        normed = (unit * gain2 + offset2).astype(BF16)
        s.normed2_t[b] = normed.T
        top = cotangent[rows, :].astype(F32) * valid_rows(start, RF)
        s.fob[...] += col_sum(top)
        top = top.astype(BF16)
        s.top_t[b] = top.T
        for c in range(units // step_units):
            cols = slice(c * step_units, (c + 1) * step_units)
            pre = mm(normed, ffn_in[:, cols]) + s.ffn_in_bias[:, cols]
            share = 0.5 + 0.5 * lax.erf(pre * SQRT_HALF)
            active = (pre * share).astype(BF16)
            s.active[rows, cols] = active
            slope = share + pre * (jnp.exp(-0.5 * pre * pre) * INV_SQRT_2PI)
            grad_pre = (mm_nt(top, ffn_out[cols, :]) * slope).astype(BF16)
            s.grad_pre[rows, cols] = grad_pre
            s.fib[:, cols] += col_sum(grad_pre.astype(F32))
            back = mm_nt(grad_pre, ffn_in[:, cols])
            onward = mm(active, ffn_out[cols, :])
            if c == 0:
                s.gn2_send[rows, :] = back
                s.out_send[rows, :] = onward
            else:
                s.gn2_send[rows, :] += back
                s.out_send[rows, :] += onward
        gn2_copy(b).start()

    feed(0)

    def grad_chunk(left_t, right):
        total = mm(left_t[0], right[0:RF])
        for b in range(1, slots // RF):
            total += mm(left_t[b], right[b * RF : (b + 1) * RF])
        return total

    per = units // CW
    first_wo, first_in = 2 * per, 2 * per + 2
    chunks = first_in + 3

    def hold(total, chunk, begun=False):
        if not ring:
            s.g_full[chunk] = s.g_full[chunk] + total if begun else total
            return
        slot = chunk % SLOTS
        parts = total.reshape(8, 2, 48, CW)
        even, odd = parts[:, 0], parts[:, 1]
        near = jnp.where(core == 0, even, odd).reshape(2, 2, 2, 48, CW)
        far = jnp.where(core == 0, odd, even).reshape(2, 2, 2, 48, CW)
        s.g_own[chunk] = s.g_own[chunk] + near if begun else near
        s.g_send[slot] = s.g_send[slot] + far if begun else far

    def keep(total, chunk, begun=False):
        if ring and chunk >= SLOTS:
            core_copy(chunk - SLOTS).wait_send()
            pl.semaphore_wait(s.free.at[chunk % SLOTS], 1)
        hold(total, chunk, begun)
        if ring:
            core_copy(chunk).start()

    def core_copy(chunk):
        slot = chunk % SLOTS
        return remote(s.g_send.at[slot], s.core_recv.at[slot], s.gc_sem, chunk, core_peer)

    def first_copy(chunk):
        own = s.g_own.at[chunk]
        if chunk in Z_FIRST:
            return remote(own.at[:, 1 - z_low_at], s.first_recv.at[chunk], s.g1_sem, chunk, z_low)
        return remote(own.at[:, :, 1 - x_at], s.first_recv.at[chunk], s.g1_sem, chunk, x_peer)

    def second_copy(chunk):
        own = s.g_own.at[chunk]
        into = s.late_recv.at[chunk, 0:2]
        if chunk in Z_FIRST:
            return remote(own.at[1 - z_high_at, z_low_at], into, s.g2_sem, chunk, z_high)
        return remote(own.at[:, 1 - z_low_at, x_at], into, s.g2_sem, chunk, z_low)

    def third_copy(chunk):
        own = s.g_own.at[chunk]
        into = s.late_recv.at[chunk, 2]
        if chunk in Z_FIRST:
            return remote(own.at[z_high_at, z_low_at, 1 - x_at], into, s.g3_sem, chunk, x_peer)
        return remote(own.at[1 - z_high_at, z_low_at, x_at], into, s.g3_sem, chunk, z_high)

    def core_done(*which):
        for chunk in which if ring else ():
            core_copy(chunk).wait_recv()
            s.g_own[chunk] = s.g_own[chunk] + s.core_recv[chunk % SLOTS]
            if chunk + SLOTS < chunks:
                pl.semaphore_signal(s.free.at[chunk % SLOTS], inc=1, device_id=core_peer, device_id_type=MESH)
            first_copy(chunk).start()

    def first_done(*which):
        for chunk in which if ring else ():
            first_copy(chunk).wait_recv()
            if chunk in Z_FIRST:
                s.g_own[chunk, :, z_low_at] = s.g_own[chunk, :, z_low_at] + s.first_recv[chunk]
            else:
                s.g_own[chunk, :, :, x_at] = s.g_own[chunk, :, :, x_at] + s.first_recv[chunk]
            second_copy(chunk).start()

    def second_done(*which):
        for chunk in which if ring else ():
            second_copy(chunk).wait_recv()
            if chunk in Z_FIRST:
                s.g_own[chunk, z_high_at, z_low_at] = s.g_own[chunk, z_high_at, z_low_at] + s.late_recv[chunk, 0:2]
            else:
                s.g_own[chunk, :, z_low_at, x_at] = s.g_own[chunk, :, z_low_at, x_at] + s.late_recv[chunk, 0:2]
            third_copy(chunk).start()

    def results(at, near, far):
        return pltpu.make_async_copy(near, far, s.out_dma.at[at])

    def grad_result(chunk):
        if chunk < per:
            far = far_ffn_out_grad.at[:, chunk * CW : (chunk + 1) * CW]
        elif chunk < 2 * per:
            far = far_ffn_in_grad.at[:, (chunk - per) * CW : (chunk - per + 1) * CW]
        else:
            far = far_attn_in_grad.at[chunk - first_in]
        return results(2 * blocks + 1 + chunk, s.grads.at[chunk], far)

    def third_done(*which):
        for chunk in which if ring else ():
            third_copy(chunk).wait_recv()
            s.grads[chunk] = s.g_own[chunk, z_high_at, z_low_at, x_at] + s.late_recv[chunk, 2]
            if not first_wo <= chunk < first_in:
                grad_result(chunk).start()

    def wo_grad_copy():
        return remote(s.grads.at[first_wo + 1 - ten], s.wo_grad_recv, s.wo_grad_sem, 0, y_peer)

    def wo_grad_done():
        wo_grad_copy().wait_recv()
        s.wo_grad[...] = s.grads[first_wo + ten] + s.wo_grad_recv[...]
        wo_grad_result().start()

    def wo_grad_result():
        return results(2 * blocks + 1 + first_wo, s.wo_grad, far_attn_out_grad)

    def own_rows(j):
        start = pl.multiple_of((2 * j + ten) * RB, RB)
        rows = pl.ds(start, RB)
        gn2_copy(j).wait_recv()
        grad_normed = s.gn2_send[rows, :] + s.gn2_recv[j]
        unit, scale = norm_stats(s.middle[rows, :])
        s.n2[0:1, :] += col_sum(grad_normed * unit)
        s.n2[1:2, :] += col_sum(grad_normed)
        top = cotangent[rows, :].astype(F32) * valid_rows(start, RB)
        grad_middle = top + norm_back(grad_normed, unit, scale, gain2)
        s.grad_middle[j] = grad_middle
        grad_attended = grad_middle.astype(BF16)
        s.grad_ctx_send[j] = mm_nt(grad_attended, s.wo[far_half, :]).astype(BF16).astype(F32)
        grad_ctx_copy(j).start()
        s.aob[...] += col_sum(grad_attended.astype(F32))
        s.grad_att_t[j] = grad_attended.T
        grad_context = mm_nt(grad_attended, attn_out[...]).astype(BF16)
        for p in range(pairs):
            s.grad_ctx[j, p] = grad_context[:, p * 128 : (p + 1) * 128]

    def far_rows(j):
        grad_ctx_copy(j).wait_recv()
        for p in range(pairs):
            s.grad_ctx[2 + j, p] = s.grad_ctx_recv[j, :, p * 128 : (p + 1) * 128].astype(BF16)

    def out_grad(c, b):
        return mm(s.top_t[b], s.active[b * RF : (b + 1) * RF, c * CW : (c + 1) * CW])

    def keep_in(c):
        keep(grad_chunk(s.normed2_t, s.grad_pre.at[:, c * CW : (c + 1) * CW]), per + c)

    def keep_wo(h):
        total = None
        for j in range(2):
            rows = pl.ds(pl.multiple_of((2 * j + ten) * RB, RB), RB)
            context = jnp.concatenate([s.ctx[h * pairs + p, rows, :] for p in range(pairs)], axis=1)
            term = mm(s.grad_att_t[j], context)
            total = term if total is None else total + term
        keep(total, first_wo + h)

    for c in range(per):
        hold(out_grad(c, 0), c)
    feed(1)
    for c in range(per):
        keep(out_grad(c, 1), c, True)
        if c >= 2:
            core_done(c - 2)
    own_rows(0)
    for c in range(2):
        keep_in(c)
        core_done(2 + c)
    own_rows(1)
    for i in range(blocks):
        out_copy(i).start()
    for c in range(2, per):
        keep_in(c)
        core_done(2 + c)
    for h in range(2):
        keep_wo(h)
        core_done(per + 2 + h)

    s.grad_k[...] = jnp.zeros_like(s.grad_k)
    s.grad_v[...] = jnp.zeros_like(s.grad_v)
    s.grad_table[...] = jnp.zeros_like(s.grad_table)
    flip_row = lax.broadcasted_iota(jnp.int32, (2 * RB, 2 * RB), 0)
    flip_col = lax.broadcasted_iota(jnp.int32, (2 * RB, 2 * RB), 1)
    same_half = (flip_row < RB) == (flip_col < RB)
    local_row = lax.rem(flip_row, RB)
    local_col = lax.rem(flip_col, RB)
    flip = (same_half & (local_row + local_col == RB - 1)).astype(BF16)

    def attend_back(step, i):
        start = pl.multiple_of(i * RB, RB)
        rows = pl.ds(start, RB)

        def pair_step(p, carry):
            qs = stack(s.q[p, rows, :])
            gs = stack(s.grad_ctx[step, p])
            low = s.probs[p, i]
            s.grad_v[p] += mm_tn(low, gs)
            shares = low.astype(F32)
            grad_shares = mm_nt(gs, s.v[p])
            inner = jnp.sum(grad_shares * shares, axis=-1, keepdims=True)
            grad_scores = (shares * (grad_shares - inner)).astype(BF16)
            s.grad_k[p] += mm_tn(grad_scores, qs)
            grad_q = mm(grad_scores, s.k[p])
            flipped = mm(flip, grad_scores)
            wide = jnp.concatenate([flipped, jnp.zeros((2 * RB, RB), F32)], axis=1)
            spread = jnp.concatenate(
                [
                    pltpu.roll(wide[:RB], 0, 1, stride=1, stride_axis=0),
                    pltpu.roll(wide[RB:], 0, 1, stride=1, stride_axis=0),
                ],
                axis=0,
            ).astype(BF16)
            q_flipped = mm(flip, qs).astype(BF16)
            s.grad_table[table_rows_of(i), :] += mm_tn(spread, q_flipped)
            turned = mm(spread, s.table[table_rows_of(i), :])
            high = turned.astype(BF16)
            rest = (turned - high.astype(F32)).astype(BF16)
            grad_q = unstack(grad_q + (mm(flip, high) + mm(flip, rest))).astype(BF16)
            cols = pl.ds(pl.multiple_of(p * 128, 128), 128)
            s.grad_pre[rows, cols] = (grad_q.astype(F32) * head_scale).astype(BF16)
            return carry

        lax.fori_loop(0, pairs, pair_step, 0)

    attend_back(0, ten)
    core_done(first_wo, first_wo + 1)
    first_done(0, 1)
    attend_back(1, 2 + ten)
    first_done(2)
    far_rows(0)
    attend_back(2, 1 - ten)
    first_done(4, 3)
    second_done(0, 1, 2)
    far_rows(1)
    attend_back(3, 3 - ten)
    first_done(5)
    second_done(4, 3)
    third_done(0)

    for p in range(pairs):
        at = local + p * 128
        s.grad_pre[:, at : at + 128] = s.grad_k[p].astype(BF16)
        at += local
        s.grad_pre[:, at : at + 128] = s.grad_v[p].astype(BF16)
    for j in range(2):
        gn2_copy(j).wait_send()

    def back_copy(i):
        rows = pl.ds(pl.multiple_of(i * RB, RB), RB)
        return remote(s.gn2_send.at[rows], s.gn1_recv.at[rows], s.gn1_sem, i, y_peer)

    def project_back(b, carry):
        start = pl.multiple_of(b * RF, RF)
        rows = pl.ds(start, RF)
        total = (
            mm_nt(s.grad_pre[rows, 0:local], attn_in[0])
            + mm_nt(s.grad_pre[rows, local : 2 * local], attn_in[1])
            + mm_nt(s.grad_pre[rows, 2 * local : 3 * local], attn_in[2])
        )
        unit, scale = norm_stats(hidden[rows, :].astype(F32))
        s.gn2_send[rows, :] = norm_back(total, unit, scale, gain1)
        own = pl.ds(pl.multiple_of(start + ten * RB, RB), RB)
        s.gn2_send[own, :] += s.grad_middle[b]
        for j in range(RF // RB):
            back_copy(b * (RF // RB) + j).start()
        s.n1[0:1, :] += col_sum(total * unit)
        s.n1[1:2, :] += col_sum(total)
        return carry

    lax.fori_loop(0, slots // RF, project_back, 0)

    def put(at, row):
        for j in range(row.shape[1] // 128):
            g_vec_acc[at + j : at + j + 1, :] = row[:, j * 128 : (j + 1) * 128]

    put(V_N1G, s.n1[0:1, :])
    put(V_N1B, s.n1[1:2, :])
    put(V_N2G, s.n2[0:1, :])
    put(V_N2B, s.n2[1:2, :])
    put(V_AOB, s.aob[...])
    put(V_FOB, s.fob[...])
    put(V_FIB, s.fib[...])
    put(V_AIB, col_sum(s.grad_pre[:, 0:local].astype(F32)))
    put(V_AIB + pairs, col_sum(s.grad_pre[:, 2 * local : 3 * local].astype(F32)))
    grad_rel = None
    rest = s.grad_table[...]
    for part in range(3):
        piece16 = rest.astype(BF16)
        term = mm_tn(pick, piece16)
        grad_rel = term if part == 0 else grad_rel + term
        rest = rest - piece16.astype(F32)
    grad_rel = grad_rel + pltpu.roll(grad_rel, HD, 1)
    fold = lax.broadcasted_iota(jnp.int32, (reach, 128), 1) < HD
    g_vec_acc[V_REL : V_REL + reach, :] = jnp.where(fold, grad_rel[:reach], grad_rel[reach:])

    def vec_step(step, peer, count):
        rows = pl.ds(0, count)
        return remote(s.vec_send.at[step, rows], s.vec_recv.at[step, rows], s.vec_sem, step, peer)

    def share(step, peer, count):
        s.vec_send[step, 0:count] = g_vec_acc[0:count, :]
        vec_step(step, peer, count).start()

    def merge(step, peer, count):
        vec_step(step, peer, count).wait_recv()
        g_vec_acc[0:count, :] = s.vec_send[step, 0:count] + s.vec_recv[step, 0:count]

    if ring:
        share(1, core_peer, VROWS)

    for c in range(3):
        keep(grad_chunk(s.normed_t, s.grad_pre.at[:, c * local : (c + 1) * local]), first_in + c)

    def finish_out(i, carry):
        start = pl.multiple_of(i * RB, RB)
        rows = pl.ds(start, RB)
        out_copy(i).wait_recv()
        branch = s.out_send[rows, :] + s.out_recv[rows, :]
        total = s.middle[rows, :] + (branch + out_bias2)
        output[rows, :] = (total * valid_rows(start, RB)).astype(BF16)
        results(i, output.at[rows], far_output.at[rows]).start()
        return carry

    def finish_hidden(i, carry):
        rows = pl.ds(pl.multiple_of(i * RB, RB), RB)
        back_copy(i).wait_recv()
        grad_hidden[rows, :] = (s.gn2_send[rows, :] + s.gn1_recv[rows, :]).astype(BF16)
        results(blocks + i, grad_hidden.at[rows], far_grad_hidden.at[rows]).start()
        return carry

    vec_out = results(2 * blocks, g_vec_acc, far_vec)
    if ring:
        second_done(5)
        first_done(6)
        core_done(first_in, first_in + 1, first_in + 2)
        merge(1, core_peer, VROWS)
        share(2, z_low, VROWS)
        first_done(7)
        second_done(6)
        third_done(2, 3)
        merge(2, z_low, VROWS)
        share(3, z_high, VROWS)
        lax.fori_loop(0, blocks, finish_out, 0)
        first_done(8)
        second_done(7)
        third_done(5)
        merge(3, z_high, VROWS)
        share(4, x_peer, VROWS)
        first_done(9)
        second_done(8)
        third_done(6, 7)
        first_done(10)
        second_done(9)
        third_done(8, 1, 4)
        first_done(11)
        second_done(10)
        third_done(9)
        wo_grad_copy().start()
        first_done(12)
        second_done(11)
        third_done(10)
        merge(4, x_peer, VROWS)
        share(0, y_peer, YROWS)
        second_done(12)
        third_done(11)
        lax.fori_loop(0, blocks - 1, finish_hidden, 0)
        third_done(12)
        finish_hidden(blocks - 1, 0)
        wo_grad_done()
        merge(0, y_peer, YROWS)
        vec_out.start()
    else:
        share(0, y_peer, YROWS)
        lax.fori_loop(0, blocks, finish_out, 0)
        lax.fori_loop(0, blocks, finish_hidden, 0)
        merge(0, y_peer, YROWS)
        vec_out.start()

    wo_y().wait_send()
    if ring:
        wo_x().wait_send()
        wo_z().wait_send()
        wo_xz().wait_send()
        wo_core(True).wait_send()
        wo_core(False).wait_send()

    def sent(i, carry):
        for p in range(pairs):
            ctx_copy(i, p).wait_send()
        out_copy(i).wait_send()
        back_copy(i).wait_send()
        return carry

    lax.fori_loop(0, blocks, sent, 0)
    vec_step(0, y_peer, YROWS).wait_send()
    if ring:
        for step, peer in enumerate((core_peer, z_low, z_high, x_peer)):
            vec_step(step + 1, peer, VROWS).wait_send()
        for c in range(chunks):
            if c >= chunks - SLOTS:
                core_copy(c).wait_send()
            first_copy(c).wait_send()
            second_copy(c).wait_send()
            third_copy(c).wait_send()
            if not first_wo <= c < first_in:
                grad_result(c).wait()
        wo_grad_copy().wait_send()
        wo_grad_result().wait()
    for j in range(2):
        grad_ctx_copy(j).wait_send()
    for i in range(blocks):
        rows = slice(i * RB, (i + 1) * RB)
        results(i, output.at[rows], far_output.at[rows]).wait()
        results(blocks + i, grad_hidden.at[rows], far_grad_hidden.at[rows]).wait()
    vec_out.wait()


def scratch_of(ring, slots, width, local, units, chunks):
    pairs = local // 128
    blocks = slots // RB
    halves = slots // RF
    vm, dma = pltpu.VMEM, pltpu.SemaphoreType.DMA
    shapes = dict(
        hidden=vm((slots, width), BF16),
        attn_in=vm((3, width, local), BF16),
        attn_out=vm((local, width), BF16),
        ffn_in=vm((width, units), BF16),
        ffn_out=vm((units, width), BF16),
        cotangent=vm((slots, width), BF16),
        output=vm((slots, width), BF16),
        grad_hidden=vm((slots, width), BF16),
        in_s=dma((6,)),
        out_dma=dma((2 * blocks + 1 + chunks,)),
        normed_t=vm((halves, width, RF), BF16),
        q=vm((pairs, slots, 128), BF16),
        k=vm((pairs, slots, 128), BF16),
        v=vm((pairs, slots, 128), BF16),
        table=vm((2 * slots, 128), BF16),
        probs=vm((pairs, blocks, 2 * RB, slots), BF16),
        ctx=vm((2 * pairs, slots, 128), BF16),
        ctx_send=vm((pairs, slots, 128), F32),
        ctx_recv=vm((pairs, slots, 128), F32),
        wo=vm((2 * local, width), BF16),
        wo_stage=vm((local // 8, width) if ring else (local, width), F32),
        wo_recv=vm((2, 2, 2, local // 8, width) if ring else (local, width), F32),
        middle=vm((slots, width), F32),
        normed2_t=vm((halves, width, RF), BF16),
        top_t=vm((halves, width, RF), BF16),
        active=vm((slots, units), BF16),
        grad_pre=vm((slots, units), BF16),
        gn2_send=vm((slots, width), F32),
        gn2_recv=vm((blocks // 2, RB, width), F32),
        gn1_recv=vm((slots, width), F32),
        out_send=vm((slots, width), F32),
        out_recv=vm((slots, width), F32),
        grad_middle=vm((blocks // 2, RB, width), F32),
        grad_att_t=vm((blocks // 2, width, RB), BF16),
        grad_ctx_send=vm((blocks // 2, RB, local), F32),
        grad_ctx_recv=vm((blocks // 2, RB, local), F32),
        grad_ctx=vm((blocks, pairs, RB, 128), BF16),
        grad_k=vm((pairs, slots, 128), F32),
        grad_v=vm((pairs, slots, 128), F32),
        grad_table=vm((2 * slots, 128), F32),
        vec=vm((VROWS, 128), F32),
        vec_send=vm((5 if ring else 1, VROWS, 128), F32),
        vec_recv=vm((5 if ring else 1, VROWS, 128), F32),
        fib=vm((1, units), F32),
        fob=vm((1, width), F32),
        aob=vm((1, width), F32),
        n1=vm((2, width), F32),
        n2=vm((2, width), F32),
        ffn_in_bias=vm((1, units), F32),
        free=pltpu.SemaphoreType.REGULAR((SLOTS,)),
        wo_sem=dma((2, 8)),
        ctx_sem=dma((2, blocks * pairs)),
        gn2_sem=dma((2, blocks // 2)),
        grad_ctx_sem=dma((2, blocks // 2)),
        gn1_sem=dma((2, blocks)),
        out_sem=dma((2, blocks)),
        vec_sem=dma((2, 5)),
    )
    if ring:
        shapes.update(
            g_own=vm((chunks, 2, 2, 2, 48, CW), F32),
            g_send=vm((SLOTS, 2, 2, 2, 48, CW), F32),
            core_recv=vm((SLOTS, 2, 2, 2, 48, CW), F32),
            first_recv=vm((chunks, 2, 2, 48, CW), F32),
            late_recv=vm((chunks, 3, 48, CW), F32),
            grads=vm((chunks, 48, CW), F32),
            wo_grad=vm((48, CW), F32),
            wo_grad_recv=vm((48, CW), F32),
            gc_sem=dma((2, chunks)),
            g1_sem=dma((2, chunks)),
            g2_sem=dma((2, chunks)),
            g3_sem=dma((2, chunks)),
            wo_grad_sem=dma((2, 1)),
        )
    return shapes


def place(
    output_in, grad_hidden_in, attn_in_in, attn_out_in, ffn_in_in, ffn_out_in, vec,
    output, grad_hidden, g_attn_in, g_attn_out_t, g_ffn_in, g_ffn_out_t,
    g_attn_in_bias, g_rel_t, g_attn_out_bias, g_norm1_gain, g_norm1_bias, g_norm2_gain, g_norm2_bias,
    g_ffn_in_bias, g_ffn_out_bias,
):
    for ref, source in (
        (output, output_in), (grad_hidden, grad_hidden_in), (g_attn_in, attn_in_in), (g_attn_out_t, attn_out_in),
        (g_ffn_in, ffn_in_in), (g_ffn_out_t, ffn_out_in),
    ):
        ref[...] = source[...]
    for ref, at in (
        (g_attn_out_bias, V_AOB), (g_norm1_gain, V_N1G), (g_norm1_bias, V_N1B), (g_norm2_gain, V_N2G),
        (g_norm2_bias, V_N2B), (g_ffn_in_bias, V_FIB), (g_ffn_out_bias, V_FOB),
    ):
        ref[...] = vec[at : at + ref.shape[0], :]
    local = g_attn_in_bias.shape[1]
    for k in range(2):
        at = V_AIB + k * (local // 128)
        g_attn_in_bias[k : k + 1, :] = jnp.concatenate(
            [vec[at + j : at + j + 1, :] for j in range(local // 128)], axis=1
        )
    reach = g_rel_t.shape[1] // 2
    turned = vec[V_REL : V_REL + reach, :].T
    g_rel_t[...] = jnp.concatenate([turned[:HD], turned[HD:]], axis=1)


def on_device(
    ring,
    hidden, lengths, attn_in, attn_in_bias, rel_table, attn_out, attn_out_bias,
    norm1_gain, norm1_bias, norm2_gain, norm2_bias,
    ffn_in, ffn_in_bias, ffn_out, ffn_out_bias, cotangent,
):
    slots, width = hidden.shape
    local = attn_out.shape[0]
    units = ffn_in.shape[1]
    table_rows = rel_table.shape[0]
    chunks = 2 * units // CW + 5
    rows = width // 16
    shape = jax.ShapeDtypeStruct
    shapes = scratch_of(ring, slots, width, local, units, chunks)
    names = tuple(shapes)
    outs = [
        shape((slots, width), BF16), shape((slots, width), BF16), shape((3, rows, local), F32), shape((rows, local), F32),
        shape((rows, units), F32), shape((rows, units), F32), shape((VROWS, 128), F32),
    ]
    far = pl.BlockSpec(memory_space=pl.ANY)
    near = pl.BlockSpec(memory_space=pltpu.VMEM)
    out_specs = [far] * 7
    if not ring:
        names = (FULL,) + names
        outs.append(shape((chunks, width, CW), F32))
        out_specs.append(near)

    def lanes(vector):
        return vector.reshape(vector.shape[0] // 128, 128)

    def unlanes(array):
        return array.reshape(array.shape[0] * 128)

    results = pl.pallas_call(
        partial(body, ring, names),
        out_shape=outs,
        in_specs=[pl.BlockSpec(memory_space=pltpu.SMEM)] + [near] * 9 + [far] * 6,
        out_specs=out_specs,
        scratch_shapes=list(shapes.values()),
        compiler_params=pltpu.CompilerParams(
            collective_id=0, has_side_effects=True, vmem_limit_bytes=64 * 1024 * 1024
        ),
    )(
        lengths, attn_in_bias, rel_table.T, lanes(attn_out_bias), lanes(norm1_gain), lanes(norm1_bias),
        lanes(norm2_gain), lanes(norm2_bias), lanes(ffn_in_bias), lanes(ffn_out_bias),
        hidden, attn_in, attn_out, ffn_in, ffn_out, cotangent,
    )
    if ring:
        vector = shape((width // 128, 128), F32)
        placed = pl.pallas_call(
            place,
            out_shape=outs[:6] + [
                shape((2, local), F32), shape((HD, table_rows), F32), vector, vector, vector, vector, vector,
                shape((units // 128, 128), F32), vector,
            ],
            in_specs=[near] * 7,
            out_specs=[near] * 15,
        )(*results)
        (
            output, grad_hidden, g_attn_in, g_attn_out_t, g_ffn_in, g_ffn_out_t, g_attn_in_bias, g_rel_t,
            g_attn_out_bias, n1g, n1b, n2g, n2b, g_ffn_in_bias, g_ffn_out_bias,
        ) = placed
        return (
            output, grad_hidden, g_attn_in, g_attn_in_bias, g_rel_t.T, g_attn_out_t.T, unlanes(g_attn_out_bias),
            unlanes(n1g), unlanes(n1b), unlanes(n2g), unlanes(n2b),
            g_ffn_in, unlanes(g_ffn_in_bias), g_ffn_out_t.T, unlanes(g_ffn_out_bias),
        )
    output, grad_hidden, vec, full = results[0], results[1], results[6], results[7]
    per = units // CW
    wide = jnp.swapaxes(full[: 2 * per].reshape(2, per, width, CW), 1, 2).reshape(2, width, units)

    def scatter(value, dim, axis="dp"):
        return lax.psum_scatter(value, axis, scatter_dimension=dim, tiled=True)

    g_ffn_out = scatter(wide[0].T, 1)
    g_ffn_in = scatter(wide[1], 0)
    g_attn_out = scatter(scatter(full[2 * per : 2 * per + 2], 0, "tensor")[0].T, 1)
    g_attn_in = scatter(full[2 * per + 2 : 2 * per + 5], 1)
    vec = lax.psum(vec, "dp")

    def row(at, count=width):
        return unlanes(vec[at : at + count // 128])

    rel_pairs = vec[V_REL : V_REL + table_rows // 2]
    grad_rel = jnp.concatenate([rel_pairs[:, :HD], rel_pairs[:, HD:]], axis=0)
    return (
        output, grad_hidden, g_attn_in,
        row(V_AIB, 2 * local).reshape(2, local), grad_rel, g_attn_out, row(V_AOB),
        row(V_N1G), row(V_N1B), row(V_N2G), row(V_N2B),
        g_ffn_in, row(V_FIB, units), g_ffn_out, row(V_FOB),
    )


def solution(mesh):
    ring = mesh.shape["dp"] == 16
    return jax.shard_map(
        partial(on_device, ring),
        mesh=mesh,
        in_specs=(
            P("dp", None), P("dp"), P(None, None, "tensor"), P(None, "tensor"), P(),
            P("tensor", None), P(), P(), P(), P(), P(),
            P(None, "tensor"), P("tensor"), P("tensor", None), P(), P("dp", None),
        ),
        out_specs=(
            P("dp", None), P("dp", None), P(None, "dp", "tensor"), P(None, "tensor"), P(),
            P("tensor", "dp"), P(), P(), P(), P(), P(),
            P("dp", "tensor"), P("tensor"), P("tensor", "dp"), P(),
        ),
        check_vma=False,
    )
```

time: 142 us -> 132 us (0.930)
  Pallas kernels: 141 us -> 131 us
    pallas_call x1, Pallas kernels: 138 us -> 127 us  [on_device(): pl.pallas_call(partial(body, ring, names), out_shape=outs, in_specs=[pl.B...]
where the time goes in v2:
time: 132 us
  Pallas kernels  131 us (99%)
  between operations  1.48 us (1%)
    pallas_call x1, Pallas kernels, on_device(): pl.pallas_call(partial(body, ring, names), out_shape=outs, in_specs=[pl.B...  127 us
    pallas_call x1, Pallas kernels, on_device(): pl.pallas_call(place, out_shape=outs[:6] + [shape((2, local), F32), shape...  3.24 us

profile of v2, /device:TPU:0, one launch (start us, length us, event | category | flops | bytes accessed | tf_op | source)
XLA Modules:
  0.0 132.2 jit_solution(12741220671257593966)
XLA Ops:
  1.3 127.5 %shard_map.271 = (bf16[512,768]{1,0:T(8,128)(2,1)}, bf16[512,768]{1,0:T(8,128)(2,1)}, f32[3,48,384]{2,1,0:T(8,128)}, f32[48,384]{1,0:T(8,128)}, f32[48,1536]{1,0...) custom-call(s32[1]{0:T(128)S(6)} %copy.31.lengths, bf16[2,384]{1,0:T(2,128)(2,1)} %attn_in_bias.1, ...), custom_call_target="tpu_custom_call" | custom-call | tf_op jit(solution)/shard_map/pallas_call | solution.py:886
  128.8 3.2 %shard_map.272 = (bf16[512,768]{1,0:T(8,128)(2,1)}, bf16[512,768]{1,0:T(8,128)(2,1)}, f32[3,48,384]{2,1,0:T(8,128)}, f32[48,384]{1,0:T(8,128)}, f32[48,1536]{1,0...) custom-call(bf16[512,768]{1,0:T(8,128)(2,1)} %get-tuple-element.37.o, ...), custom_call_target="tpu_custom_call" | custom-call | tf_op jit(solution)/shard_map/pallas_call | solution.py:902

commit v3 on v2

--- a/solution.py
+++ b/solution.py
@@ -17,6 +17,7 @@
 RF = 256
 CW = 384
 FULL = "g_full"
+OUT_AT, IN_AT, WO_AT, QKV_AT = (0, 1, 2, 3), (4, 5, 8, 9), (6, 7), (10, 11, 12)
 Z_FIRST = (1, 4)
 SLOTS = 4
 MESH = pl.DeviceIdType.MESH
@@ -65,10 +66,23 @@
 YROWS, VROWS = 192, 216
 
 
+def vec_place(row):
+    part, at = (row // 24, row % 24) if row < YROWS else ((row - YROWS) // 3, 24 + (row - YROWS) % 3)
+    return part // 4, part // 2 % 2, part % 2, at
+
+
+def vec_rows(vec, first, count):
+    found = []
+    for row in range(first, first + count):
+        a, b, c, at = vec_place(row)
+        found.append(vec[a, b, c, at : at + 1, :])
+    return found
+
+
 def body(
     ring, names,
-    lengths, attn_in_bias, rel_table_t, attn_out_bias, norm1_gain, norm1_bias, norm2_gain, norm2_bias,
-    ffn_in_bias, ffn_out_bias, far_hidden, far_attn_in, far_attn_out, far_ffn_in, far_ffn_out, far_cotangent,
+    lengths, far_attn_in_bias, far_rel_table_t, far_attn_out_bias, far_norm1_gain, far_norm1_bias, far_norm2_gain,
+    far_norm2_bias, far_ffn_in_bias, far_ffn_out_bias, far_hidden, far_attn_in, far_attn_out, far_ffn_in, far_ffn_out, far_cotangent,
     far_output, far_grad_hidden, far_attn_in_grad, far_attn_out_grad, far_ffn_in_grad, far_ffn_out_grad, far_vec,
     *scratch,
 ):
@@ -82,6 +96,12 @@
     bring_attn_out = bring(0, s.attn_out, far_attn_out)
     bring_hidden = bring(1, s.hidden, far_hidden)
     bring_attn_in = bring(2, s.attn_in, far_attn_in)
+    small = (
+        (s.attn_in_bias, far_attn_in_bias), (s.rel_table_t, far_rel_table_t), (s.attn_out_bias, far_attn_out_bias),
+        (s.norm1_gain, far_norm1_gain), (s.norm1_bias, far_norm1_bias), (s.norm2_gain, far_norm2_gain),
+        (s.norm2_bias, far_norm2_bias), (s.ffn_in_bias16, far_ffn_in_bias), (s.ffn_out_bias, far_ffn_out_bias),
+    )
+    bring_small = [bring(6 + k, near, far) for k, (near, far) in enumerate(small)]
     hidden, attn_in, attn_out = s.hidden, s.attn_in, s.attn_out
     cotangent, ffn_in, ffn_out = s.cotangent, s.ffn_in, s.ffn_out
     output, grad_hidden = s.output, s.grad_hidden
@@ -89,7 +109,7 @@
     local = attn_out.shape[0]
     pairs = local // 128
     units = ffn_in.shape[1]
-    table_rows = rel_table_t.shape[1]
+    table_rows = s.rel_table_t.shape[1]
     reach = table_rows // 2
     blocks = slots // RB
     ext = slots + RB
@@ -157,19 +177,21 @@
         value = ref[...].astype(F32)
         return jnp.concatenate([value[j : j + 1] for j in range(value.shape[0])], axis=1)
 
-    bias_q = attn_in_bias[0:1, :].astype(F32)
-    bias_v = attn_in_bias[1:2, :].astype(F32)
-    gain1, offset1 = flat(norm1_gain), flat(norm1_bias)
-    gain2, offset2 = flat(norm2_gain), flat(norm2_bias)
-    out_bias1, out_bias2 = flat(attn_out_bias), flat(ffn_out_bias)
-    s.ffn_in_bias[...] = flat(ffn_in_bias)
+    for copy in bring_small:
+        copy.wait()
+    bias_q = s.attn_in_bias[0:1, :].astype(F32)
+    bias_v = s.attn_in_bias[1:2, :].astype(F32)
+    gain1, offset1 = flat(s.norm1_gain), flat(s.norm1_bias)
+    gain2, offset2 = flat(s.norm2_gain), flat(s.norm2_bias)
+    out_bias1, out_bias2 = flat(s.attn_out_bias), flat(s.ffn_out_bias)
+    s.ffn_in_bias[...] = flat(s.ffn_in_bias16)
     seq_len = lengths[0]
 
     ext_rows = 2 * slots
     distance = slots - 1 - lax.broadcasted_iota(jnp.int32, (ext_rows, table_rows), 0)
     bucket = jnp.clip(distance, -reach, reach - 1) + reach
     pick = (bucket == lax.broadcasted_iota(jnp.int32, (ext_rows, table_rows), 1)).astype(BF16)
-    rel_t = rel_table_t[...]
+    rel_t = s.rel_table_t[...]
     s.table[...] = mm_nt(pick, jnp.concatenate([rel_t, rel_t], axis=0)).astype(BF16)
 
     def project(i, carry):
@@ -280,8 +302,7 @@
         rows = pl.ds(pl.multiple_of(i * RB, RB), RB)
         return remote(s.out_send.at[rows], s.out_recv.at[rows], s.out_sem, i, y_peer)
 
-    g_vec_acc = s.vec
-    g_vec_acc[...] = jnp.zeros_like(g_vec_acc)
+    s.vec[...] = jnp.zeros_like(s.vec)
     s.fib[...] = jnp.zeros_like(s.fib)
     s.fob[...] = jnp.zeros_like(s.fob)
     s.aob[...] = jnp.zeros_like(s.aob)
@@ -337,8 +358,7 @@
         return total
 
     per = units // CW
-    first_wo, first_in = 2 * per, 2 * per + 2
-    chunks = first_in + 3
+    chunks = 2 * per + 5
 
     def hold(total, chunk, begun=False):
         if not ring:
@@ -414,31 +434,33 @@
         return pltpu.make_async_copy(near, far, s.out_dma.at[at])
 
     def grad_result(chunk):
-        if chunk < per:
-            far = far_ffn_out_grad.at[:, chunk * CW : (chunk + 1) * CW]
-        elif chunk < 2 * per:
-            far = far_ffn_in_grad.at[:, (chunk - per) * CW : (chunk - per + 1) * CW]
+        if chunk in OUT_AT:
+            c = OUT_AT.index(chunk)
+            far = far_ffn_out_grad.at[:, c * CW : (c + 1) * CW]
+        elif chunk in IN_AT:
+            c = IN_AT.index(chunk)
+            far = far_ffn_in_grad.at[:, c * CW : (c + 1) * CW]
         else:
-            far = far_attn_in_grad.at[chunk - first_in]
+            far = far_attn_in_grad.at[QKV_AT.index(chunk)]
         return results(2 * blocks + 1 + chunk, s.grads.at[chunk], far)
 
     def third_done(*which):
         for chunk in which if ring else ():
             third_copy(chunk).wait_recv()
             s.grads[chunk] = s.g_own[chunk, z_high_at, z_low_at, x_at] + s.late_recv[chunk, 2]
-            if not first_wo <= chunk < first_in:
+            if chunk not in WO_AT:
                 grad_result(chunk).start()
 
     def wo_grad_copy():
-        return remote(s.grads.at[first_wo + 1 - ten], s.wo_grad_recv, s.wo_grad_sem, 0, y_peer)
+        return remote(s.grads.at[WO_AT[0] + 1 - ten], s.wo_grad_recv, s.wo_grad_sem, 0, y_peer)
 
     def wo_grad_done():
         wo_grad_copy().wait_recv()
-        s.wo_grad[...] = s.grads[first_wo + ten] + s.wo_grad_recv[...]
+        s.wo_grad[...] = s.grads[WO_AT[0] + ten] + s.wo_grad_recv[...]
         wo_grad_result().start()
 
     def wo_grad_result():
-        return results(2 * blocks + 1 + first_wo, s.wo_grad, far_attn_out_grad)
+        return results(2 * blocks + 1 + WO_AT[0], s.wo_grad, far_attn_out_grad)
 
     def own_rows(j):
         start = pl.multiple_of((2 * j + ten) * RB, RB)
@@ -469,7 +491,7 @@
         return mm(s.top_t[b], s.active[b * RF : (b + 1) * RF, c * CW : (c + 1) * CW])
 
     def keep_in(c):
-        keep(grad_chunk(s.normed2_t, s.grad_pre.at[:, c * CW : (c + 1) * CW]), per + c)
+        keep(grad_chunk(s.normed2_t, s.grad_pre.at[:, c * CW : (c + 1) * CW]), IN_AT[c])
 
     def keep_wo(h):
         total = None
@@ -478,7 +500,7 @@
             context = jnp.concatenate([s.ctx[h * pairs + p, rows, :] for p in range(pairs)], axis=1)
             term = mm(s.grad_att_t[j], context)
             total = term if total is None else total + term
-        keep(total, first_wo + h)
+        keep(total, WO_AT[h])
 
     for c in range(per):
         hold(out_grad(c, 0), c)
@@ -494,12 +516,12 @@
     own_rows(1)
     for i in range(blocks):
         out_copy(i).start()
-    for c in range(2, per):
-        keep_in(c)
-        core_done(2 + c)
     for h in range(2):
         keep_wo(h)
-        core_done(per + 2 + h)
+        core_done(4 + h)
+    for c in range(2):
+        keep_in(2 + c)
+        core_done(6 + c)
 
     s.grad_k[...] = jnp.zeros_like(s.grad_k)
     s.grad_v[...] = jnp.zeros_like(s.grad_v)
@@ -548,7 +570,7 @@
         lax.fori_loop(0, pairs, pair_step, 0)
 
     attend_back(0, ten)
-    core_done(first_wo, first_wo + 1)
+    core_done(8, 9)
     first_done(0, 1)
     attend_back(1, 2 + ten)
     first_done(2)
@@ -586,8 +608,6 @@
         s.gn2_send[rows, :] = norm_back(total, unit, scale, gain1)
         own = pl.ds(pl.multiple_of(start + ten * RB, RB), RB)
         s.gn2_send[own, :] += s.grad_middle[b]
-        for j in range(RF // RB):
-            back_copy(b * (RF // RB) + j).start()
         s.n1[0:1, :] += col_sum(total * unit)
         s.n1[1:2, :] += col_sum(total)
         return carry
@@ -596,7 +616,8 @@
 
     def put(at, row):
         for j in range(row.shape[1] // 128):
-            g_vec_acc[at + j : at + j + 1, :] = row[:, j * 128 : (j + 1) * 128]
+            a, b, c, i = vec_place(at + j)
+            s.vec[a, b, c, i : i + 1, :] = row[:, j * 128 : (j + 1) * 128]
 
     put(V_N1G, s.n1[0:1, :])
     put(V_N1B, s.n1[1:2, :])
@@ -616,25 +637,43 @@
         rest = rest - piece16.astype(F32)
     grad_rel = grad_rel + pltpu.roll(grad_rel, HD, 1)
     fold = lax.broadcasted_iota(jnp.int32, (reach, 128), 1) < HD
-    g_vec_acc[V_REL : V_REL + reach, :] = jnp.where(fold, grad_rel[:reach], grad_rel[reach:])
-
-    def vec_step(step, peer, count):
-        rows = pl.ds(0, count)
-        return remote(s.vec_send.at[step, rows], s.vec_recv.at[step, rows], s.vec_sem, step, peer)
-
-    def share(step, peer, count):
-        s.vec_send[step, 0:count] = g_vec_acc[0:count, :]
-        vec_step(step, peer, count).start()
-
-    def merge(step, peer, count):
-        vec_step(step, peer, count).wait_recv()
-        g_vec_acc[0:count, :] = s.vec_send[step, 0:count] + s.vec_recv[step, 0:count]
+    packed = jnp.where(fold, grad_rel[:reach], grad_rel[reach:])
+    done = 0
+    while done < reach:
+        a, b, c, at = vec_place(V_REL + done)
+        count = min(24 - at, reach - done)
+        s.vec[a, b, c, at : at + count, :] = packed[done : done + count]
+        done += count
+
+    def vec_send(src, dst, at, peer):
+        return remote(src, dst, s.vec_sem, at, peer)
 
     if ring:
-        share(1, core_peer, VROWS)
+        own_vec = s.vec.at[core, z_low_at, z_high_at]
+        vec_core = vec_send(s.vec.at[1 - core], s.vec_half, 0, core_peer)
+        vec_low = vec_send(s.vec.at[core, 1 - z_low_at], s.vec_quarter, 1, z_low)
+        vec_high = vec_send(s.vec.at[core, z_low_at, 1 - z_high_at], s.vec_eighth.at[0], 2, z_high)
+        vec_y = vec_send(own_vec.at[0:24], s.vec_eighth.at[1, 0:24], 3, y_peer)
+        vec_x = vec_send(own_vec, s.vec_eighth.at[2], 4, x_peer)
+        all_high, all_low, all_core = (
+            vec_send(part, part, 5 + k, peer)
+            for k, (part, peer) in enumerate(
+                (
+                    (s.vec_all.at[core, z_low_at, z_high_at], z_high),
+                    (s.vec_all.at[core, z_low_at], z_low),
+                    (s.vec_all.at[core], core_peer),
+                )
+            )
+        )
+        vec_core.start()
+    else:
+        vec_y = vec_send(s.vec.at[:, :, :, 0:24], s.vec_half, 0, y_peer)
+        vec_y.start()
+    back_copy(0).start()
+    back_copy(1).start()
 
     for c in range(3):
-        keep(grad_chunk(s.normed_t, s.grad_pre.at[:, c * local : (c + 1) * local]), first_in + c)
+        keep(grad_chunk(s.normed_t, s.grad_pre.at[:, c * local : (c + 1) * local]), QKV_AT[c])
 
     def finish_out(i, carry):
         start = pl.multiple_of(i * RB, RB)
@@ -653,94 +692,101 @@
         results(blocks + i, grad_hidden.at[rows], far_grad_hidden.at[rows]).start()
         return carry
 
-    vec_out = results(2 * blocks, g_vec_acc, far_vec)
+    def sent():
+        wo_y().wait_send()
+        for i in range(blocks):
+            for p in range(pairs):
+                ctx_copy(i, p).wait_send()
+            out_copy(i).wait_send()
+            rows = slice(i * RB, (i + 1) * RB)
+            results(i, output.at[rows], far_output.at[rows]).wait()
+        for j in range(2):
+            grad_ctx_copy(j).wait_send()
+        if ring:
+            for copy in (wo_x(), wo_z(), wo_xz(), wo_core(True), wo_core(False), wo_grad_copy(), vec_core, vec_low, vec_high):
+                copy.wait_send()
+            wo_grad_result().wait()
+            for c in range(chunks):
+                if c >= chunks - SLOTS:
+                    core_copy(c).wait_send()
+                first_copy(c).wait_send()
+                second_copy(c).wait_send()
+                third_copy(c).wait_send()
+                if c not in WO_AT:
+                    grad_result(c).wait()
+
+    vec_out = results(2 * blocks, s.vec_all if ring else s.vec, far_vec)
     if ring:
+        first_done(6)
         second_done(5)
-        first_done(6)
-        core_done(first_in, first_in + 1, first_in + 2)
-        merge(1, core_peer, VROWS)
-        share(2, z_low, VROWS)
+        vec_core.wait_recv()
+        s.vec[core] = s.vec[core] + s.vec_half[...]
+        vec_low.start()
+        core_done(*QKV_AT)
         first_done(7)
         second_done(6)
         third_done(2, 3)
-        merge(2, z_low, VROWS)
-        share(3, z_high, VROWS)
+        first_done(8)
+        vec_low.wait_recv()
+        s.vec[core, z_low_at] = s.vec[core, z_low_at] + s.vec_quarter[...]
+        vec_high.start()
+        second_done(7)
+        third_done(5, 6)
+        first_done(9)
+        vec_high.wait_recv()
+        own_vec[...] = own_vec[...] + s.vec_eighth[0]
+        vec_y.start()
+        third_done(7)
+        wo_grad_copy().start()
+        back_copy(2).start()
+        back_copy(3).start()
+        second_done(8)
         lax.fori_loop(0, blocks, finish_out, 0)
-        first_done(8)
-        second_done(7)
-        third_done(5)
-        merge(3, z_high, VROWS)
-        share(4, x_peer, VROWS)
-        first_done(9)
-        second_done(8)
-        third_done(6, 7)
         first_done(10)
         second_done(9)
-        third_done(8, 1, 4)
+        third_done(8)
+        vec_y.wait()
+        own_vec[0:24] = own_vec[0:24] + s.vec_eighth[1, 0:24]
+        vec_x.start()
         first_done(11)
+        third_done(9, 1, 4)
         second_done(10)
-        third_done(9)
-        wo_grad_copy().start()
+        wo_grad_done()
         first_done(12)
         second_done(11)
         third_done(10)
-        merge(4, x_peer, VROWS)
-        share(0, y_peer, YROWS)
+        vec_x.wait()
+        s.vec_all[core, z_low_at, z_high_at] = own_vec[...] + s.vec_eighth[2]
+        all_high.start()
         second_done(12)
         third_done(11)
-        lax.fori_loop(0, blocks - 1, finish_hidden, 0)
+        all_high.wait_recv()
+        all_low.start()
         third_done(12)
-        finish_hidden(blocks - 1, 0)
-        wo_grad_done()
-        merge(0, y_peer, YROWS)
-        vec_out.start()
+        all_low.wait_recv()
+        all_core.start()
+        sent()
+        all_core.wait_recv()
     else:
-        share(0, y_peer, YROWS)
+        back_copy(2).start()
+        back_copy(3).start()
+        vec_y.wait()
+        s.vec[:, :, :, 0:24] = s.vec[:, :, :, 0:24] + s.vec_half[...]
         lax.fori_loop(0, blocks, finish_out, 0)
-        lax.fori_loop(0, blocks, finish_hidden, 0)
-        merge(0, y_peer, YROWS)
-        vec_out.start()
-
-    wo_y().wait_send()
-    if ring:
-        wo_x().wait_send()
-        wo_z().wait_send()
-        wo_xz().wait_send()
-        wo_core(True).wait_send()
-        wo_core(False).wait_send()
-
-    def sent(i, carry):
-        for p in range(pairs):
-            ctx_copy(i, p).wait_send()
-        out_copy(i).wait_send()
-        back_copy(i).wait_send()
-        return carry
-
-    lax.fori_loop(0, blocks, sent, 0)
-    vec_step(0, y_peer, YROWS).wait_send()
-    if ring:
-        for step, peer in enumerate((core_peer, z_low, z_high, x_peer)):
-            vec_step(step + 1, peer, VROWS).wait_send()
-        for c in range(chunks):
-            if c >= chunks - SLOTS:
-                core_copy(c).wait_send()
-            first_copy(c).wait_send()
-            second_copy(c).wait_send()
-            third_copy(c).wait_send()
-            if not first_wo <= c < first_in:
-                grad_result(c).wait()
-        wo_grad_copy().wait_send()
-        wo_grad_result().wait()
-    for j in range(2):
-        grad_ctx_copy(j).wait_send()
+        sent()
+    vec_out.start()
+    lax.fori_loop(0, blocks, finish_hidden, 0)
     for i in range(blocks):
         rows = slice(i * RB, (i + 1) * RB)
-        results(i, output.at[rows], far_output.at[rows]).wait()
+        back_copy(i).wait_send()
         results(blocks + i, grad_hidden.at[rows], far_grad_hidden.at[rows]).wait()
     vec_out.wait()
-
-
-def scratch_of(ring, slots, width, local, units, chunks):
+    if ring:
+        for copy in (all_high, all_low, all_core):
+            copy.wait_send()
+
+
+def scratch_of(ring, slots, width, local, units, table_rows, chunks):
     pairs = local // 128
     blocks = slots // RB
     halves = slots // RF
@@ -754,7 +800,7 @@
         cotangent=vm((slots, width), BF16),
         output=vm((slots, width), BF16),
         grad_hidden=vm((slots, width), BF16),
-        in_s=dma((6,)),
+        in_s=dma((15,)),
         out_dma=dma((2 * blocks + 1 + chunks,)),
         normed_t=vm((halves, width, RF), BF16),
         q=vm((pairs, slots, 128), BF16),
@@ -786,9 +832,17 @@
         grad_k=vm((pairs, slots, 128), F32),
         grad_v=vm((pairs, slots, 128), F32),
         grad_table=vm((2 * slots, 128), F32),
-        vec=vm((VROWS, 128), F32),
-        vec_send=vm((5 if ring else 1, VROWS, 128), F32),
-        vec_recv=vm((5 if ring else 1, VROWS, 128), F32),
+        attn_in_bias=vm((2, local), BF16),
+        rel_table_t=vm((HD, table_rows), BF16),
+        attn_out_bias=vm((width // 128, 128), BF16),
+        norm1_gain=vm((width // 128, 128), BF16),
+        norm1_bias=vm((width // 128, 128), BF16),
+        norm2_gain=vm((width // 128, 128), BF16),
+        norm2_bias=vm((width // 128, 128), BF16),
+        ffn_in_bias16=vm((units // 128, 128), BF16),
+        ffn_out_bias=vm((width // 128, 128), BF16),
+        vec=vm((2, 2, 2, 32, 128), F32),
+        vec_half=vm((2, 2, 32, 128) if ring else (2, 2, 2, 24, 128), F32),
         fib=vm((1, units), F32),
         fob=vm((1, width), F32),
         aob=vm((1, width), F32),
@@ -802,7 +856,7 @@
         grad_ctx_sem=dma((2, blocks // 2)),
         gn1_sem=dma((2, blocks)),
         out_sem=dma((2, blocks)),
-        vec_sem=dma((2, 5)),
+        vec_sem=dma((2, 8)),
     )
     if ring:
         shapes.update(
@@ -812,6 +866,9 @@
             first_recv=vm((chunks, 2, 2, 48, CW), F32),
             late_recv=vm((chunks, 3, 48, CW), F32),
             grads=vm((chunks, 48, CW), F32),
+            vec_quarter=vm((2, 32, 128), F32),
+            vec_eighth=vm((3, 32, 128), F32),
+            vec_all=vm((2, 2, 2, 32, 128), F32),
             wo_grad=vm((48, CW), F32),
             wo_grad_recv=vm((48, CW), F32),
             gc_sem=dma((2, chunks)),
@@ -823,31 +880,32 @@
     return shapes
 
 
-def place(
-    output_in, grad_hidden_in, attn_in_in, attn_out_in, ffn_in_in, ffn_out_in, vec,
-    output, grad_hidden, g_attn_in, g_attn_out_t, g_ffn_in, g_ffn_out_t,
-    g_attn_in_bias, g_rel_t, g_attn_out_bias, g_norm1_gain, g_norm1_bias, g_norm2_gain, g_norm2_bias,
-    g_ffn_in_bias, g_ffn_out_bias,
-):
-    for ref, source in (
-        (output, output_in), (grad_hidden, grad_hidden_in), (g_attn_in, attn_in_in), (g_attn_out_t, attn_out_in),
-        (g_ffn_in, ffn_in_in), (g_ffn_out_t, ffn_out_in),
-    ):
-        ref[...] = source[...]
-    for ref, at in (
-        (g_attn_out_bias, V_AOB), (g_norm1_gain, V_N1G), (g_norm1_bias, V_N1B), (g_norm2_gain, V_N2G),
-        (g_norm2_bias, V_N2B), (g_ffn_in_bias, V_FIB), (g_ffn_out_bias, V_FOB),
-    ):
-        ref[...] = vec[at : at + ref.shape[0], :]
-    local = g_attn_in_bias.shape[1]
+def place(*refs):
+    ins, outs, held, small, sems = refs[:7], refs[7:22], refs[22:29], refs[29:38], refs[38]
+    bring = [pltpu.make_async_copy(far, near, sems.at[k]) for k, (far, near) in enumerate(zip(ins, held))]
+    write = [
+        pltpu.make_async_copy(near, far, sems.at[7 + k]) for k, (near, far) in enumerate(zip(held[:6] + small, outs))
+    ]
+    for copy in bring[::-1]:
+        copy.start()
+    bring[6].wait()
+    vec = held[6]
+    g_attn_in_bias, g_rel_t = small[:2]
+    for ref, at in zip(small[2:], (V_AOB, V_N1G, V_N1B, V_N2G, V_N2B, V_FIB, V_FOB)):
+        ref[...] = jnp.concatenate(vec_rows(vec, at, ref.shape[0]), axis=0)
+    count = g_attn_in_bias.shape[1] // 128
     for k in range(2):
-        at = V_AIB + k * (local // 128)
-        g_attn_in_bias[k : k + 1, :] = jnp.concatenate(
-            [vec[at + j : at + j + 1, :] for j in range(local // 128)], axis=1
-        )
+        g_attn_in_bias[k : k + 1, :] = jnp.concatenate(vec_rows(vec, V_AIB + k * count, count), axis=1)
     reach = g_rel_t.shape[1] // 2
-    turned = vec[V_REL : V_REL + reach, :].T
+    turned = jnp.concatenate(vec_rows(vec, V_REL, reach), axis=0).T
     g_rel_t[...] = jnp.concatenate([turned[:HD], turned[HD:]], axis=1)
+    for copy in write[6:]:
+        copy.start()
+    for k in range(6):
+        bring[k].wait()
+        write[k].start()
+    for copy in write:
+        copy.wait()
 
 
 def on_device(
@@ -863,11 +921,11 @@
     chunks = 2 * units // CW + 5
     rows = width // 16
     shape = jax.ShapeDtypeStruct
-    shapes = scratch_of(ring, slots, width, local, units, chunks)
+    shapes = scratch_of(ring, slots, width, local, units, table_rows, chunks)
     names = tuple(shapes)
     outs = [
         shape((slots, width), BF16), shape((slots, width), BF16), shape((3, rows, local), F32), shape((rows, local), F32),
-        shape((rows, units), F32), shape((rows, units), F32), shape((VROWS, 128), F32),
+        shape((rows, units), F32), shape((rows, units), F32), shape((2, 2, 2, 32, 128), F32),
     ]
     far = pl.BlockSpec(memory_space=pl.ANY)
     near = pl.BlockSpec(memory_space=pltpu.VMEM)
@@ -886,7 +944,7 @@
     results = pl.pallas_call(
         partial(body, ring, names),
         out_shape=outs,
-        in_specs=[pl.BlockSpec(memory_space=pltpu.SMEM)] + [near] * 9 + [far] * 6,
+        in_specs=[pl.BlockSpec(memory_space=pltpu.SMEM)] + [far] * 15,
         out_specs=out_specs,
         scratch_shapes=list(shapes.values()),
         compiler_params=pltpu.CompilerParams(
@@ -899,14 +957,17 @@
     )
     if ring:
         vector = shape((width // 128, 128), F32)
+        small = [
+            shape((2, local), F32), shape((HD, table_rows), F32), vector, vector, vector, vector, vector,
+            shape((units // 128, 128), F32), vector,
+        ]
         placed = pl.pallas_call(
             place,
-            out_shape=outs[:6] + [
-                shape((2, local), F32), shape((HD, table_rows), F32), vector, vector, vector, vector, vector,
-                shape((units // 128, 128), F32), vector,
-            ],
-            in_specs=[near] * 7,
-            out_specs=[near] * 15,
+            out_shape=outs[:6] + small,
+            in_specs=[far] * 7,
+            out_specs=[far] * 15,
+            scratch_shapes=[pltpu.VMEM(array.shape, array.dtype) for array in outs + small]
+            + [pltpu.SemaphoreType.DMA((22,))],
         )(*results)
         (
             output, grad_hidden, g_attn_in, g_attn_out_t, g_ffn_in, g_ffn_out_t, g_attn_in_bias, g_rel_t,
@@ -918,22 +979,23 @@
             g_ffn_in, unlanes(g_ffn_in_bias), g_ffn_out_t.T, unlanes(g_ffn_out_bias),
         )
     output, grad_hidden, vec, full = results[0], results[1], results[6], results[7]
-    per = units // CW
-    wide = jnp.swapaxes(full[: 2 * per].reshape(2, per, width, CW), 1, 2).reshape(2, width, units)
+
+    def wide(which):
+        return jnp.concatenate([full[c] for c in which], axis=1)
 
     def scatter(value, dim, axis="dp"):
         return lax.psum_scatter(value, axis, scatter_dimension=dim, tiled=True)
 
-    g_ffn_out = scatter(wide[0].T, 1)
-    g_ffn_in = scatter(wide[1], 0)
-    g_attn_out = scatter(scatter(full[2 * per : 2 * per + 2], 0, "tensor")[0].T, 1)
-    g_attn_in = scatter(full[2 * per + 2 : 2 * per + 5], 1)
+    g_ffn_out = scatter(wide(OUT_AT).T, 1)
+    g_ffn_in = scatter(wide(IN_AT), 0)
+    g_attn_out = scatter(scatter(full[WO_AT[0] : WO_AT[1] + 1], 0, "tensor")[0].T, 1)
+    g_attn_in = scatter(full[QKV_AT[0] : QKV_AT[2] + 1], 1)
     vec = lax.psum(vec, "dp")
 
     def row(at, count=width):
-        return unlanes(vec[at : at + count // 128])
-
-    rel_pairs = vec[V_REL : V_REL + table_rows // 2]
+        return unlanes(jnp.concatenate(vec_rows(vec, at, count // 128), axis=0))
+
+    rel_pairs = jnp.concatenate(vec_rows(vec, V_REL, table_rows // 2), axis=0)
     grad_rel = jnp.concatenate([rel_pairs[:, :HD], rel_pairs[:, HD:]], axis=0)
     return (
         output, grad_hidden, g_attn_in,

time: 132 us -> 130 us (0.985)
  Pallas kernels: 131 us -> 128 us
    pallas_call x1, Pallas kernels: 127 us -> 125 us  [on_device(): pl.pallas_call(partial(body, ring, names), out_shape=outs, in_specs=[pl.B...]
where the time goes in v3:
time: 130 us
  Pallas kernels  128 us (98%)
  between operations  1.49 us (1%)
    pallas_call x1, Pallas kernels, on_device(): pl.pallas_call(partial(body, ring, names), out_shape=outs, in_specs=[pl.B...  125 us
    pallas_call x1, Pallas kernels, on_device(): pl.pallas_call(place, out_shape=outs[:6] + small, in_specs=[far] * 7, out...  3.36 us

profile of v3, /device:TPU:0, one launch (start us, length us, event | category | flops | bytes accessed | tf_op | source)
XLA Modules:
  0.0 129.6 jit_solution(368832880088490774)
XLA Ops:
  1.3 124.8 %shard_map.271 = (bf16[512,768]{1,0:T(8,128)(2,1)}, bf16[512,768]{1,0:T(8,128)(2,1)}, f32[3,48,384]{2,1,0:T(8,128)}, f32[48,384]{1,0:T(8,128)}, f32[48,1536]{1,0...) custom-call(s32[1]{0:T(128)S(6)} %copy.31.lengths, bf16[2,384]{1,0:T(2,128)(2,1)} %far_attn_in_bias.1, ...), custom_call_target="tpu_custom_call" | custom-call | tf_op jit(solution)/shard_map/pallas_call | solution.py:944
  126.1 3.4 %shard_map.272 = (bf16[512,768]{1,0:T(8,128)(2,1)}, bf16[512,768]{1,0:T(8,128)(2,1)}, f32[3,48,384]{2,1,0:T(8,128)}, f32[48,384]{1,0:T(8,128)}, f32[48,1536]{1,0...) custom-call(bf16[512,768]{1,0:T(8,128)(2,1)} %get-tuple-element.37.r, ...), custom_call_target="tpu_custom_call" | custom-call | tf_op jit(solution)/shard_map/pallas_call | solution.py:964

commit v4 on v3

--- a/solution.py
+++ b/solution.py
@@ -18,7 +18,7 @@
 CW = 384
 FULL = "g_full"
 OUT_AT, IN_AT, WO_AT, QKV_AT = (0, 1, 2, 3), (4, 5, 8, 9), (6, 7), (10, 11, 12)
-Z_FIRST = (1, 4)
+Z_FIRST = (0, 2, 3)
 SLOTS = 4
 MESH = pl.DeviceIdType.MESH
 F32 = jnp.float32
@@ -291,12 +291,9 @@
     def valid_rows(start, count):
         return (lax.broadcasted_iota(jnp.int32, (count, 1), 0) + start < seq_len).astype(F32)
 
-    def gn2_copy(j):
-        rows = pl.ds(pl.multiple_of((2 * j + 1 - ten) * RB, RB), RB)
-        return remote(s.gn2_send.at[rows], s.gn2_recv.at[j], s.gn2_sem, j, y_peer)
-
-    def grad_ctx_copy(j):
-        return remote(s.grad_ctx_send.at[j], s.grad_ctx_recv.at[j], s.grad_ctx_sem, j, y_peer)
+    def grad_ctx_copy(i):
+        rows = pl.ds(i * RB, RB)
+        return remote(s.grad_ctx_send.at[rows], s.grad_ctx_recv.at[rows], s.grad_ctx_sem, i, y_peer)
 
     def out_copy(i):
         rows = pl.ds(pl.multiple_of(i * RB, RB), RB)
@@ -322,11 +319,12 @@
         attended = mm(lanes_of(s.ctx, rows), s.wo[...]) + out_bias1
         middle = hidden[rows, :].astype(F32) + attended
         s.middle[rows, :] = middle
-        unit, unused = norm_stats(middle)
+        unit, scale = norm_stats(middle)
         normed = (unit * gain2 + offset2).astype(BF16)
         s.normed2_t[b] = normed.T
         top = cotangent[rows, :].astype(F32) * valid_rows(start, RF)
         s.fob[...] += col_sum(top)
+        half_top = 0.5 * top
         top = top.astype(BF16)
         s.top_t[b] = top.T
         for c in range(units // step_units):
@@ -342,12 +340,29 @@
             back = mm_nt(grad_pre, ffn_in[:, cols])
             onward = mm(active, ffn_out[cols, :])
             if c == 0:
-                s.gn2_send[rows, :] = back
+                s.gn1_send[rows, :] = back
                 s.out_send[rows, :] = onward
             else:
-                s.gn2_send[rows, :] += back
+                s.gn1_send[rows, :] += back
                 s.out_send[rows, :] += onward
-        gn2_copy(b).start()
+            if b == 1:
+                for chunk in range(per):
+                    if c * step_units < (chunk + 1) * CW <= (c + 1) * step_units:
+                        keep(out_grad(chunk, 1), chunk, True)
+                if c > 0:
+                    core_done(c - 1)
+        back = s.gn1_send[rows, :]
+        s.n2[0:1, :] += col_sum(back * unit)
+        s.n2[1:2, :] += col_sum(back)
+        grad_middle = half_top + norm_back(back, unit, scale, gain2)
+        s.grad_middle[rows, :] = grad_middle
+        grad_attended = grad_middle.astype(BF16)
+        s.grad_ctx_send[rows, :] = mm_nt(grad_attended, s.wo[far_half, :])
+        for j in range(RF // RB):
+            grad_ctx_copy(b * (RF // RB) + j).start()
+        s.grad_ctx_own[rows, :] = mm_nt(grad_attended, attn_out[...])
+        s.aob[...] += col_sum(grad_attended.astype(F32))
+        s.grad_att_t[b] = grad_attended.T
 
     feed(0)
 
@@ -462,31 +477,6 @@
     def wo_grad_result():
         return results(2 * blocks + 1 + WO_AT[0], s.wo_grad, far_attn_out_grad)
 
-    def own_rows(j):
-        start = pl.multiple_of((2 * j + ten) * RB, RB)
-        rows = pl.ds(start, RB)
-        gn2_copy(j).wait_recv()
-        grad_normed = s.gn2_send[rows, :] + s.gn2_recv[j]
-        unit, scale = norm_stats(s.middle[rows, :])
-        s.n2[0:1, :] += col_sum(grad_normed * unit)
-        s.n2[1:2, :] += col_sum(grad_normed)
-        top = cotangent[rows, :].astype(F32) * valid_rows(start, RB)
-        grad_middle = top + norm_back(grad_normed, unit, scale, gain2)
-        s.grad_middle[j] = grad_middle
-        grad_attended = grad_middle.astype(BF16)
-        s.grad_ctx_send[j] = mm_nt(grad_attended, s.wo[far_half, :]).astype(BF16).astype(F32)
-        grad_ctx_copy(j).start()
-        s.aob[...] += col_sum(grad_attended.astype(F32))
-        s.grad_att_t[j] = grad_attended.T
-        grad_context = mm_nt(grad_attended, attn_out[...]).astype(BF16)
-        for p in range(pairs):
-            s.grad_ctx[j, p] = grad_context[:, p * 128 : (p + 1) * 128]
-
-    def far_rows(j):
-        grad_ctx_copy(j).wait_recv()
-        for p in range(pairs):
-            s.grad_ctx[2 + j, p] = s.grad_ctx_recv[j, :, p * 128 : (p + 1) * 128].astype(BF16)
-
     def out_grad(c, b):
         return mm(s.top_t[b], s.active[b * RF : (b + 1) * RF, c * CW : (c + 1) * CW])
 
@@ -494,28 +484,18 @@
         keep(grad_chunk(s.normed2_t, s.grad_pre.at[:, c * CW : (c + 1) * CW]), IN_AT[c])
 
     def keep_wo(h):
-        total = None
-        for j in range(2):
-            rows = pl.ds(pl.multiple_of((2 * j + ten) * RB, RB), RB)
-            context = jnp.concatenate([s.ctx[h * pairs + p, rows, :] for p in range(pairs)], axis=1)
-            term = mm(s.grad_att_t[j], context)
-            total = term if total is None else total + term
+        context = jnp.concatenate([s.ctx[h * pairs + p] for p in range(pairs)], axis=1)
+        total = grad_chunk(s.grad_att_t, context)
         keep(total, WO_AT[h])
 
     for c in range(per):
         hold(out_grad(c, 0), c)
     feed(1)
-    for c in range(per):
-        keep(out_grad(c, 1), c, True)
-        if c >= 2:
-            core_done(c - 2)
-    own_rows(0)
+    for i in range(blocks):
+        out_copy(i).start()
     for c in range(2):
         keep_in(c)
         core_done(2 + c)
-    own_rows(1)
-    for i in range(blocks):
-        out_copy(i).start()
     for h in range(2):
         keep_wo(h)
         core_done(4 + h)
@@ -533,13 +513,14 @@
     local_col = lax.rem(flip_col, RB)
     flip = (same_half & (local_row + local_col == RB - 1)).astype(BF16)
 
-    def attend_back(step, i):
-        start = pl.multiple_of(i * RB, RB)
-        rows = pl.ds(start, RB)
+    def attend_back(i):
+        rows = pl.ds(i * RB, RB)
+        grad_ctx_copy(i).wait_recv()
 
         def pair_step(p, carry):
             qs = stack(s.q[p, rows, :])
-            gs = stack(s.grad_ctx[step, p])
+            cols = pl.ds(pl.multiple_of(p * 128, 128), 128)
+            gs = stack((s.grad_ctx_own[rows, cols] + s.grad_ctx_recv[rows, cols]).astype(BF16))
             low = s.probs[p, i]
             s.grad_v[p] += mm_tn(low, gs)
             shares = low.astype(F32)
@@ -563,38 +544,29 @@
             high = turned.astype(BF16)
             rest = (turned - high.astype(F32)).astype(BF16)
             grad_q = unstack(grad_q + (mm(flip, high) + mm(flip, rest))).astype(BF16)
-            cols = pl.ds(pl.multiple_of(p * 128, 128), 128)
             s.grad_pre[rows, cols] = (grad_q.astype(F32) * head_scale).astype(BF16)
             return carry
 
         lax.fori_loop(0, pairs, pair_step, 0)
 
-    attend_back(0, ten)
+    attend_back(0)
     core_done(8, 9)
     first_done(0, 1)
-    attend_back(1, 2 + ten)
-    first_done(2)
-    far_rows(0)
-    attend_back(2, 1 - ten)
-    first_done(4, 3)
-    second_done(0, 1, 2)
-    far_rows(1)
-    attend_back(3, 3 - ten)
-    first_done(5)
-    second_done(4, 3)
-    third_done(0)
+    attend_back(1)
+    first_done(2, 4)
+    attend_back(2)
+    first_done(3, 5)
+    attend_back(3)
+    second_done(0, 1)
 
     for p in range(pairs):
         at = local + p * 128
         s.grad_pre[:, at : at + 128] = s.grad_k[p].astype(BF16)
         at += local
         s.grad_pre[:, at : at + 128] = s.grad_v[p].astype(BF16)
-    for j in range(2):
-        gn2_copy(j).wait_send()
-
     def back_copy(i):
         rows = pl.ds(pl.multiple_of(i * RB, RB), RB)
-        return remote(s.gn2_send.at[rows], s.gn1_recv.at[rows], s.gn1_sem, i, y_peer)
+        return remote(s.gn1_send.at[rows], s.gn1_recv.at[rows], s.gn1_sem, i, y_peer)
 
     def project_back(b, carry):
         start = pl.multiple_of(b * RF, RF)
@@ -605,9 +577,7 @@
             + mm_nt(s.grad_pre[rows, 2 * local : 3 * local], attn_in[2])
         )
         unit, scale = norm_stats(hidden[rows, :].astype(F32))
-        s.gn2_send[rows, :] = norm_back(total, unit, scale, gain1)
-        own = pl.ds(pl.multiple_of(start + ten * RB, RB), RB)
-        s.gn2_send[own, :] += s.grad_middle[b]
+        s.gn1_send[rows, :] = norm_back(total, unit, scale, gain1) + s.grad_middle[rows, :]
         s.n1[0:1, :] += col_sum(total * unit)
         s.n1[1:2, :] += col_sum(total)
         return carry
@@ -688,7 +658,7 @@
     def finish_hidden(i, carry):
         rows = pl.ds(pl.multiple_of(i * RB, RB), RB)
         back_copy(i).wait_recv()
-        grad_hidden[rows, :] = (s.gn2_send[rows, :] + s.gn1_recv[rows, :]).astype(BF16)
+        grad_hidden[rows, :] = (s.gn1_send[rows, :] + s.gn1_recv[rows, :]).astype(BF16)
         results(blocks + i, grad_hidden.at[rows], far_grad_hidden.at[rows]).start()
         return carry
 
@@ -698,10 +668,9 @@
             for p in range(pairs):
                 ctx_copy(i, p).wait_send()
             out_copy(i).wait_send()
+            grad_ctx_copy(i).wait_send()
             rows = slice(i * RB, (i + 1) * RB)
             results(i, output.at[rows], far_output.at[rows]).wait()
-        for j in range(2):
-            grad_ctx_copy(j).wait_send()
         if ring:
             for copy in (wo_x(), wo_z(), wo_xz(), wo_core(True), wo_core(False), wo_grad_copy(), vec_core, vec_low, vec_high):
                 copy.wait_send()
@@ -718,54 +687,59 @@
     vec_out = results(2 * blocks, s.vec_all if ring else s.vec, far_vec)
     if ring:
         first_done(6)
-        second_done(5)
+        second_done(2, 4)
+        core_done(*QKV_AT)
         vec_core.wait_recv()
         s.vec[core] = s.vec[core] + s.vec_half[...]
         vec_low.start()
-        core_done(*QKV_AT)
         first_done(7)
+        second_done(3, 5)
+        third_done(1)
+        first_done(8)
         second_done(6)
-        third_done(2, 3)
-        first_done(8)
+        third_done(4)
+        lax.fori_loop(0, blocks, finish_out, 0)
         vec_low.wait_recv()
         s.vec[core, z_low_at] = s.vec[core, z_low_at] + s.vec_quarter[...]
         vec_high.start()
+        first_done(9)
+        third_done(0)
         second_done(7)
-        third_done(5, 6)
-        first_done(9)
+        third_done(2, 5)
+        second_done(8)
+        third_done(6)
         vec_high.wait_recv()
         own_vec[...] = own_vec[...] + s.vec_eighth[0]
         vec_y.start()
+        first_done(10)
+        second_done(9)
         third_done(7)
         wo_grad_copy().start()
         back_copy(2).start()
         back_copy(3).start()
-        second_done(8)
-        lax.fori_loop(0, blocks, finish_out, 0)
-        first_done(10)
-        second_done(9)
         third_done(8)
         vec_y.wait()
         own_vec[0:24] = own_vec[0:24] + s.vec_eighth[1, 0:24]
         vec_x.start()
         first_done(11)
-        third_done(9, 1, 4)
         second_done(10)
-        wo_grad_done()
+        third_done(9)
         first_done(12)
         second_done(11)
+        third_done(3)
+        wo_grad_done()
         third_done(10)
+        second_done(12)
+        third_done(11)
         vec_x.wait()
         s.vec_all[core, z_low_at, z_high_at] = own_vec[...] + s.vec_eighth[2]
         all_high.start()
-        second_done(12)
-        third_done(11)
+        third_done(12)
         all_high.wait_recv()
         all_low.start()
-        third_done(12)
+        sent()
         all_low.wait_recv()
         all_core.start()
-        sent()
         all_core.wait_recv()
     else:
         back_copy(2).start()
@@ -819,16 +793,15 @@
         top_t=vm((halves, width, RF), BF16),
         active=vm((slots, units), BF16),
         grad_pre=vm((slots, units), BF16),
-        gn2_send=vm((slots, width), F32),
-        gn2_recv=vm((blocks // 2, RB, width), F32),
+        gn1_send=vm((slots, width), F32),
         gn1_recv=vm((slots, width), F32),
         out_send=vm((slots, width), F32),
         out_recv=vm((slots, width), F32),
-        grad_middle=vm((blocks // 2, RB, width), F32),
-        grad_att_t=vm((blocks // 2, width, RB), BF16),
-        grad_ctx_send=vm((blocks // 2, RB, local), F32),
-        grad_ctx_recv=vm((blocks // 2, RB, local), F32),
-        grad_ctx=vm((blocks, pairs, RB, 128), BF16),
+        grad_middle=vm((slots, width), F32),
+        grad_att_t=vm((halves, width, RF), BF16),
+        grad_ctx_own=vm((slots, local), F32),
+        grad_ctx_send=vm((slots, local), F32),
+        grad_ctx_recv=vm((slots, local), F32),
         grad_k=vm((pairs, slots, 128), F32),
         grad_v=vm((pairs, slots, 128), F32),
         grad_table=vm((2 * slots, 128), F32),
@@ -852,8 +825,7 @@
         free=pltpu.SemaphoreType.REGULAR((SLOTS,)),
         wo_sem=dma((2, 8)),
         ctx_sem=dma((2, blocks * pairs)),
-        gn2_sem=dma((2, blocks // 2)),
-        grad_ctx_sem=dma((2, blocks // 2)),
+        grad_ctx_sem=dma((2, blocks)),
         gn1_sem=dma((2, blocks)),
         out_sem=dma((2, blocks)),
         vec_sem=dma((2, 8)),

time: 130 us -> 125 us (0.962); the launches traced: 130 us -> 123 us
  Pallas kernels: 128 us -> 122 us
    pallas_call x1, Pallas kernels: 125 us -> 118 us  [on_device(): pl.pallas_call(partial(body, ring, names), out_shape=outs, in_specs=[pl.B...]
where the time goes in v4:
time: 125 us; the launch traced here: 123 us
  Pallas kernels  122 us (98%)
  between operations  1.49 us (1%)
    pallas_call x1, Pallas kernels, on_device(): pl.pallas_call(partial(body, ring, names), out_shape=outs, in_specs=[pl.B...  118 us
    pallas_call x1, Pallas kernels, on_device(): pl.pallas_call(place, out_shape=outs[:6] + small, in_specs=[far] * 7, out...  3.36 us

profile of v4, /device:TPU:0, one launch (start us, length us, event | category | flops | bytes accessed | tf_op | source)
XLA Modules:
  0.0 123.2 jit_solution(10722645972512253968)
XLA Ops:
  1.3 118.3 %shard_map.271 = (bf16[512,768]{1,0:T(8,128)(2,1)}, bf16[512,768]{1,0:T(8,128)(2,1)}, f32[3,48,384]{2,1,0:T(8,128)}, f32[48,384]{1,0:T(8,128)}, f32[48,1536]{1,0...) custom-call(s32[1]{0:T(128)S(6)} %copy.31.lengths, bf16[2,384]{1,0:T(2,128)(2,1)} %far_attn_in_bias.1, ...), custom_call_target="tpu_custom_call" | custom-call | tf_op jit(solution)/shard_map/pallas_call | solution.py:916
  119.6 3.4 %shard_map.272 = (bf16[512,768]{1,0:T(8,128)(2,1)}, bf16[512,768]{1,0:T(8,128)(2,1)}, f32[3,48,384]{2,1,0:T(8,128)}, f32[48,384]{1,0:T(8,128)}, f32[48,1536]{1,0...) custom-call(bf16[512,768]{1,0:T(8,128)(2,1)} %get-tuple-element.37.r, ...), custom_call_target="tpu_custom_call" | custom-call | tf_op jit(solution)/shard_map/pallas_call | solution.py:936

commit v5 on v4

--- a/solution.py
+++ b/solution.py
@@ -622,9 +622,9 @@
         own_vec = s.vec.at[core, z_low_at, z_high_at]
         vec_core = vec_send(s.vec.at[1 - core], s.vec_half, 0, core_peer)
         vec_low = vec_send(s.vec.at[core, 1 - z_low_at], s.vec_quarter, 1, z_low)
-        vec_high = vec_send(s.vec.at[core, z_low_at, 1 - z_high_at], s.vec_eighth.at[0], 2, z_high)
-        vec_y = vec_send(own_vec.at[0:24], s.vec_eighth.at[1, 0:24], 3, y_peer)
-        vec_x = vec_send(own_vec, s.vec_eighth.at[2], 4, x_peer)
+        vec_high = vec_send(s.vec.at[core, z_low_at, 1 - z_high_at], s.vec_eighth, 2, z_high)
+        vec_y = vec_send(s.vec.at[core, :, :, 0:24], s.vec_y_recv, 3, y_peer)
+        vec_x = vec_send(s.vec.at[core], s.vec_x_recv, 4, x_peer)
         all_high, all_low, all_core = (
             vec_send(part, part, 5 + k, peer)
             for k, (part, peer) in enumerate(
@@ -639,8 +639,8 @@
     else:
         vec_y = vec_send(s.vec.at[:, :, :, 0:24], s.vec_half, 0, y_peer)
         vec_y.start()
-    back_copy(0).start()
-    back_copy(1).start()
+    for i in range(blocks - 2):
+        back_copy(i).start()
 
     for c in range(3):
         keep(grad_chunk(s.normed_t, s.grad_pre.at[:, c * local : (c + 1) * local]), QKV_AT[c])
@@ -672,26 +672,28 @@
             rows = slice(i * RB, (i + 1) * RB)
             results(i, output.at[rows], far_output.at[rows]).wait()
         if ring:
-            for copy in (wo_x(), wo_z(), wo_xz(), wo_core(True), wo_core(False), wo_grad_copy(), vec_core, vec_low, vec_high):
+            for copy in (wo_x(), wo_z(), wo_xz(), wo_core(True), wo_core(False), vec_core, vec_low):
                 copy.wait_send()
-            wo_grad_result().wait()
             for c in range(chunks):
                 if c >= chunks - SLOTS:
                     core_copy(c).wait_send()
                 first_copy(c).wait_send()
-                second_copy(c).wait_send()
-                third_copy(c).wait_send()
-                if c not in WO_AT:
-                    grad_result(c).wait()
+
+    def sent_late(*which):
+        for c in which:
+            second_copy(c).wait_send()
+            third_copy(c).wait_send()
+            if c not in WO_AT:
+                grad_result(c).wait()
 
     vec_out = results(2 * blocks, s.vec_all if ring else s.vec, far_vec)
     if ring:
         first_done(6)
         second_done(2, 4)
-        core_done(*QKV_AT)
         vec_core.wait_recv()
         s.vec[core] = s.vec[core] + s.vec_half[...]
-        vec_low.start()
+        vec_x.start()
+        core_done(*QKV_AT)
         first_done(7)
         second_done(3, 5)
         third_done(1)
@@ -699,57 +701,67 @@
         second_done(6)
         third_done(4)
         lax.fori_loop(0, blocks, finish_out, 0)
-        vec_low.wait_recv()
-        s.vec[core, z_low_at] = s.vec[core, z_low_at] + s.vec_quarter[...]
-        vec_high.start()
         first_done(9)
+        vec_x.wait()
+        s.vec[core] = s.vec[core] + s.vec_x_recv[...]
+        vec_y.start()
+        back_copy(blocks - 2).start()
         third_done(0)
         second_done(7)
         third_done(2, 5)
         second_done(8)
         third_done(6)
-        vec_high.wait_recv()
-        own_vec[...] = own_vec[...] + s.vec_eighth[0]
-        vec_y.start()
         first_done(10)
         second_done(9)
         third_done(7)
         wo_grad_copy().start()
-        back_copy(2).start()
-        back_copy(3).start()
+        back_copy(blocks - 1).start()
+        vec_y.wait()
+        s.vec[core, :, :, 0:24] = s.vec[core, :, :, 0:24] + s.vec_y_recv[...]
+        vec_low.start()
         third_done(8)
-        vec_y.wait()
-        own_vec[0:24] = own_vec[0:24] + s.vec_eighth[1, 0:24]
-        vec_x.start()
         first_done(11)
         second_done(10)
         third_done(9)
+        vec_low.wait_recv()
+        s.vec[core, z_low_at] = s.vec[core, z_low_at] + s.vec_quarter[...]
+        vec_high.start()
         first_done(12)
+        finish_hidden(0, 0)
+        finish_hidden(1, 0)
         second_done(11)
         third_done(3)
+        vec_high.wait_recv()
+        s.vec_all[core, z_low_at, z_high_at] = own_vec[...] + s.vec_eighth[...]
+        all_high.start()
         wo_grad_done()
         third_done(10)
         second_done(12)
         third_done(11)
-        vec_x.wait()
-        s.vec_all[core, z_low_at, z_high_at] = own_vec[...] + s.vec_eighth[2]
-        all_high.start()
-        third_done(12)
+        sent()
         all_high.wait_recv()
         all_low.start()
-        sent()
+        sent_late(*range(chunks - 1))
+        third_done(12)
         all_low.wait_recv()
         all_core.start()
+        wo_grad_copy().wait_send()
+        vec_high.wait_send()
+        finish_hidden(2, 0)
         all_core.wait_recv()
+        vec_out.start()
+        finish_hidden(3, 0)
+        sent_late(12)
+        wo_grad_result().wait()
     else:
-        back_copy(2).start()
-        back_copy(3).start()
+        back_copy(blocks - 2).start()
+        back_copy(blocks - 1).start()
         vec_y.wait()
         s.vec[:, :, :, 0:24] = s.vec[:, :, :, 0:24] + s.vec_half[...]
         lax.fori_loop(0, blocks, finish_out, 0)
+        vec_out.start()
         sent()
-    vec_out.start()
-    lax.fori_loop(0, blocks, finish_hidden, 0)
+        lax.fori_loop(0, blocks, finish_hidden, 0)
     for i in range(blocks):
         rows = slice(i * RB, (i + 1) * RB)
         back_copy(i).wait_send()
@@ -839,7 +851,9 @@
             late_recv=vm((chunks, 3, 48, CW), F32),
             grads=vm((chunks, 48, CW), F32),
             vec_quarter=vm((2, 32, 128), F32),
-            vec_eighth=vm((3, 32, 128), F32),
+            vec_x_recv=vm((2, 2, 32, 128), F32),
+            vec_y_recv=vm((2, 2, 24, 128), F32),
+            vec_eighth=vm((32, 128), F32),
             vec_all=vm((2, 2, 2, 32, 128), F32),
             wo_grad=vm((48, CW), F32),
             wo_grad_recv=vm((48, CW), F32),

time: 125 us -> 123 us (0.984)
  no operation moved by 1% of the time
where the time goes in v5:
time: 123 us; the launch traced here: 122 us
  Pallas kernels  121 us (98%)
  between operations  1.49 us (1%)
    pallas_call x1, Pallas kernels, on_device(): pl.pallas_call(partial(body, ring, names), out_shape=outs, in_specs=[pl.B...  117 us
    pallas_call x1, Pallas kernels, on_device(): pl.pallas_call(place, out_shape=outs[:6] + small, in_specs=[far] * 7, out...  3.36 us

profile of v5, /device:TPU:0, one launch (start us, length us, event | category | flops | bytes accessed | tf_op | source)
XLA Modules:
  0.0 122.2 jit_solution(2059643081584104049)
XLA Ops:
  1.3 117.3 %shard_map.271 = (bf16[512,768]{1,0:T(8,128)(2,1)}, bf16[512,768]{1,0:T(8,128)(2,1)}, f32[3,48,384]{2,1,0:T(8,128)}, f32[48,384]{1,0:T(8,128)}, f32[48,1536]{1,0...) custom-call(s32[1]{0:T(128)S(6)} %copy.31.lengths, bf16[2,384]{1,0:T(2,128)(2,1)} %far_attn_in_bias.1, ...), custom_call_target="tpu_custom_call" | custom-call | tf_op jit(solution)/shard_map/pallas_call | solution.py:930
  118.6 3.4 %shard_map.272 = (bf16[512,768]{1,0:T(8,128)(2,1)}, bf16[512,768]{1,0:T(8,128)(2,1)}, f32[3,48,384]{2,1,0:T(8,128)}, f32[48,384]{1,0:T(8,128)}, f32[48,1536]{1,0...) custom-call(bf16[512,768]{1,0:T(8,128)(2,1)} %get-tuple-element.37.r, ...), custom_call_target="tpu_custom_call" | custom-call | tf_op jit(solution)/shard_map/pallas_call | solution.py:950
